TPU v7x, 32 devices: a whole 2x2x4 slice. The times are simulated.
32 devices in a mesh: row: 8 (over z, core), col: 4 (over y, x).
Axes of the slice: x: 2, y: 2, z: 4, core: 2. Of those that a mesh axis runs over, the one named last changes fastest.
Arguments:
- weather: bfloat16 [192, 1024, 1024], P(None, 'row', 'col'), may hold values from -6 to 6
- cotangent: bfloat16 [192, 1024, 1024], P(None, 'row', 'col'), may hold values from -6 to 6
- spectral_in: bfloat16 [2, 2, 96, 96], replicated, may hold values from -0.4375 to 0.4375
- spectral_bias: float32 [2, 2, 96], replicated, may hold values from -3 to 3
- spectral_out: bfloat16 [2, 2, 96, 96], replicated, may hold values from -1.75 to 1.75
- project_in: bfloat16 [192, 768], replicated, may hold values from -0.4375 to 0.4375
- project_out: bfloat16 [768, 192], replicated, may hold values from -0.21875 to 0.21875
Outputs:
- layer_out: bfloat16 [192, 1024, 1024], P(None, 'row', 'col')
- grad_weather: bfloat16 [192, 1024, 1024], P(None, 'row', 'col')
- grad_project_in: float32 [192, 768], replicated
- grad_project_out: float32 [768, 192], replicated
- grad_spectral_in: float32 [2, 2, 96, 96], replicated
- grad_spectral_out: float32 [2, 2, 96, 96], replicated
- grad_spectral_bias: float32 [2, 2, 96], replicated
All inputs are finite; a program needn't handle non-finite values.
Results may differ from a plain program's by a relative error of at most 0.019.
The roundings to bfloat16 on the way count: a program that leaves them out, or rounds other values in their place, can miss the bound.
Values may be sent and summed in bfloat16 or wider, within the bound.
No kernel may reach another device: no remote copies, remote signals or barrier semaphores. Data moves between devices by JAX's collectives and lax.ppermute only.
A program may use at most 512 MiB of HBM per device.

v0:
```python
import math

import jax
import jax.numpy as jnp
from jax import lax
from jax.sharding import PartitionSpec as P

H = 1024
W = 1024
NB = 2
BS = 96
KH = 512
KW = 256


epsilon = 1e-05
threshold = 0.1


def product(form, left, right):
    return jnp.einsum(form, left, right, preferred_element_type=jnp.float32)


def gelu_slope(values):
    return 0.5 * (1.0 + lax.erf(values * (1.0 / math.sqrt(2.0)))) + values * jnp.exp(
        -0.5 * values * values
    ) * (1.0 / math.sqrt(2.0 * math.pi))


def width_tables(width, kept):
    position = jnp.arange(width, dtype=jnp.int32)
    frequency = jnp.arange(kept, dtype=jnp.int32)
    phases = position[:, None] * frequency[None, :] % width
    angles = phases.astype(jnp.float32) * (2.0 * math.pi / width)
    factor = 1.0 / math.sqrt(width)
    weight = jnp.where(frequency == 0, 1.0, 2.0).astype(jnp.float32)
    cosine = jnp.cos(angles) * factor
    sine_values = -jnp.sin(angles) * factor
    return (
        cosine.astype(jnp.bfloat16),
        sine_values.astype(jnp.bfloat16),
        (cosine * weight[None, :]).astype(jnp.bfloat16),
        (sine_values * weight[None, :]).astype(jnp.bfloat16),
    )


def height_tables(height, kept):
    position = jnp.arange(height, dtype=jnp.int32)
    indices = jnp.arange(kept, dtype=jnp.int32)
    frequency = jnp.where(indices < kept // 2, indices, indices + (height - kept))
    phases = position[:, None] * frequency[None, :] % height
    angles = phases.astype(jnp.float32) * (2.0 * math.pi / height)
    factor = 1.0 / math.sqrt(height)
    return (
        (jnp.cos(angles) * factor).astype(jnp.bfloat16),
        (-jnp.sin(angles) * factor).astype(jnp.bfloat16),
    )


def width_forward(field_part, cosine_table, sine_table):
    real_part = product("crw,wk->rkc", field_part, cosine_table)
    imaginary = product("crw,wk->rkc", field_part, sine_table)
    return jnp.stack([real_part, imaginary], axis=2).astype(jnp.bfloat16)


def width_inverse(spectrum, cosine_table, sine_table):
    half_width = spectrum.shape[2] // 2
    summed = product("rkc,wk->crw", spectrum[:, :, :half_width], cosine_table)
    summed = summed + product("rkc,wk->crw", spectrum[:, :, half_width:], sine_table)
    return summed.astype(jnp.bfloat16)


def height_forward(spectrum, real_table, imaginary_table):
    half_width = spectrum.shape[2] // 2
    first_term = product("hnx,hm->mnx", spectrum, real_table)
    second = product("hnx,hm->mnx", spectrum, imaginary_table)
    return jnp.concatenate(
        [
            first_term[:, :, :half_width] - second[:, :, half_width:],
            first_term[:, :, half_width:] + second[:, :, :half_width],
        ],
        axis=2,
    )


def height_inverse(kept_modes, real_table, imaginary_table):
    half_width = kept_modes.shape[2] // 2
    first_term = product("mnx,hm->hnx", kept_modes, real_table)
    second = product("mnx,hm->hnx", kept_modes, imaginary_table)
    return jnp.concatenate(
        [
            first_term[:, :, :half_width] + second[:, :, half_width:],
            first_term[:, :, half_width:] - second[:, :, :half_width],
        ],
        axis=2,
    )


def soft_shrink(values):
    return values - threshold * jnp.tanh(values * (1.0 / threshold))


def shrink_slope(values):
    return jnp.square(jnp.tanh(values * (1.0 / threshold)))


def spectral_forward(kept_modes, spectral_in, spectral_bias, spectral_out):
    mode_count, column_count, doubled = kept_modes.shape
    pieces = kept_modes.reshape(mode_count, column_count, 2, NB, BS)
    real_input, imaginary_input = (pieces[:, :, 0], pieces[:, :, 1])
    before_real = (
        product("mnbi,bio->mnbo", real_input, spectral_in[0])
        - product("mnbi,bio->mnbo", imaginary_input, spectral_in[1])
        + spectral_bias[0]
    )
    before_imaginary = (
        product("mnbi,bio->mnbo", imaginary_input, spectral_in[0])
        + product("mnbi,bio->mnbo", real_input, spectral_in[1])
        + spectral_bias[1]
    )
    hidden_real = jax.nn.gelu(before_real, approximate=False).astype(jnp.bfloat16)
    hidden_imaginary = jax.nn.gelu(before_imaginary, approximate=False).astype(jnp.bfloat16)
    second_real = product("mnbi,bio->mnbo", hidden_real, spectral_out[0]) - product(
        "mnbi,bio->mnbo", hidden_imaginary, spectral_out[1]
    )
    second_imaginary = product("mnbi,bio->mnbo", hidden_imaginary, spectral_out[0]) + product(
        "mnbi,bio->mnbo", hidden_real, spectral_out[1]
    )
    shrunk = jnp.stack([soft_shrink(second_real), soft_shrink(second_imaginary)], axis=2)
    shrunk = shrunk.reshape(mode_count, column_count, doubled).astype(jnp.bfloat16)
    return (
        shrunk,
        (
            before_real,
            before_imaginary,
            hidden_real,
            hidden_imaginary,
            second_real,
            second_imaginary,
        ),
    )


def spectral_backward(gradient, kept_modes, saved, spectral_in, spectral_out):
    mode_count, column_count, doubled = gradient.shape
    grad_pieces = gradient.reshape(mode_count, column_count, 2, NB, BS)
    pieces = kept_modes.reshape(mode_count, column_count, 2, NB, BS)
    real_input, imaginary_input = (pieces[:, :, 0], pieces[:, :, 1])
    before_real, before_imaginary, hidden_real, hidden_imaginary, second_real, second_imaginary = (
        saved
    )
    keep_real = (grad_pieces[:, :, 0] * shrink_slope(second_real)).astype(jnp.bfloat16)
    keep_imaginary = (grad_pieces[:, :, 1] * shrink_slope(second_imaginary)).astype(jnp.bfloat16)
    back_real = product("mnbo,bio->mnbi", keep_real, spectral_out[0]) + product(
        "mnbo,bio->mnbi", keep_imaginary, spectral_out[1]
    )
    back_imaginary = product("mnbo,bio->mnbi", keep_imaginary, spectral_out[0]) - product(
        "mnbo,bio->mnbi", keep_real, spectral_out[1]
    )
    out_real = product("mnbi,mnbo->bio", hidden_real, keep_real) + product(
        "mnbi,mnbo->bio", hidden_imaginary, keep_imaginary
    )
    out_imaginary = product("mnbi,mnbo->bio", hidden_real, keep_imaginary) - product(
        "mnbi,mnbo->bio", hidden_imaginary, keep_real
    )
    gate_real = (back_real * gelu_slope(before_real)).astype(jnp.bfloat16)
    gate_imaginary = (back_imaginary * gelu_slope(before_imaginary)).astype(jnp.bfloat16)
    in_real = product("mnbi,mnbo->bio", real_input, gate_real) + product(
        "mnbi,mnbo->bio", imaginary_input, gate_imaginary
    )
    in_imaginary = product("mnbi,mnbo->bio", real_input, gate_imaginary) - product(
        "mnbi,mnbo->bio", imaginary_input, gate_real
    )
    bias_grad = jnp.stack(
        [
            jnp.sum(gate_real.astype(jnp.float32), axis=(0, 1)),
            jnp.sum(gate_imaginary.astype(jnp.float32), axis=(0, 1)),
        ]
    )
    input_real = product("mnbo,bio->mnbi", gate_real, spectral_in[0]) + product(
        "mnbo,bio->mnbi", gate_imaginary, spectral_in[1]
    )
    input_imaginary = product("mnbo,bio->mnbi", gate_imaginary, spectral_in[0]) - product(
        "mnbo,bio->mnbi", gate_real, spectral_in[1]
    )
    grad_modes = jnp.stack([input_real, input_imaginary], axis=2)
    grad_modes = grad_modes.reshape(mode_count, column_count, doubled).astype(jnp.bfloat16)
    return (
        grad_modes,
        jnp.stack([in_real, in_imaginary]),
        jnp.stack([out_real, out_imaginary]),
        bias_grad,
    )


def layer_norm(flat_field):
    centred = flat_field - jnp.mean(flat_field, axis=0, keepdims=True)
    variance = jnp.mean(centred * centred, axis=0, keepdims=True)
    inverse_spread = lax.rsqrt(variance + epsilon)
    return (centred * inverse_spread, inverse_spread)


def norm_backward(normed, inverse_spread, gradient):
    mean_grad = jnp.mean(gradient, axis=0, keepdims=True)
    mean_cross = jnp.mean(gradient * normed, axis=0, keepdims=True)
    return inverse_spread * (gradient - mean_grad - normed * mean_cross)


def token_block(weather, normed_in, filtered, cotangent, project_in, project_out):
    channels = weather.shape[0]
    summed = (
        weather.astype(jnp.float32) + normed_in.astype(jnp.float32) + filtered.astype(jnp.float32)
    )
    flat_sum = summed.reshape(channels, -1)
    normed, inverse_spread = layer_norm(flat_sum)
    normed_low = normed.astype(jnp.bfloat16)
    before = product("cn,ch->hn", normed_low, project_in)
    hidden = jax.nn.gelu(before, approximate=False).astype(jnp.bfloat16)
    output = (flat_sum + product("hn,hc->cn", hidden, project_out)).astype(jnp.bfloat16)
    flat_cot = cotangent.reshape(channels, -1)
    back_hidden = product("cn,hc->hn", flat_cot, project_out)
    back_before = (back_hidden * gelu_slope(before)).astype(jnp.bfloat16)
    grad_out = product("hn,cn->hc", hidden, flat_cot)
    grad_in = product("cn,hn->ch", normed_low, back_before)
    back_normed = product("hn,ch->cn", back_before, project_in)
    grad_sum = flat_cot.astype(jnp.float32) + norm_backward(normed, inverse_spread, back_normed)
    return (output.reshape(weather.shape), grad_sum.reshape(weather.shape), grad_in, grad_out)


def back_to_cells(field_part):
    return lax.all_to_all(field_part, "col", split_axis=2, concat_axis=1, tiled=True)


def local_spectrum(field_part, cosine_table, sine_table):
    channels = field_part.shape[0]
    shaped = width_forward(field_part, cosine_table, sine_table)
    return shaped.reshape(shaped.shape[0], shaped.shape[1], 2 * channels)


def to_modes(spectrum):
    return lax.all_to_all(spectrum, ("row", "col"), split_axis=1, concat_axis=0, tiled=True)


def to_rows(spectrum):
    return lax.all_to_all(spectrum, ("row", "col"), split_axis=0, concat_axis=1, tiled=True)


def body(weather, cotangent, spectral_in, spectral_bias, spectral_out, project_in, project_out):
    cosine, sine_table, cosine_weighted, sine_weighted = width_tables(W, KW)
    real_table, imaginary_table = height_tables(H, KH)
    channels = weather.shape[0]
    field_now, cot_now = (
        lax.all_to_all(weather, "col", split_axis=1, concat_axis=2, tiled=True),
        lax.all_to_all(cotangent, "col", split_axis=1, concat_axis=2, tiled=True),
    )
    normed_first, spread_first = layer_norm(field_now.astype(jnp.float32).reshape(channels, -1))
    normed_in = normed_first.astype(jnp.bfloat16).reshape(field_now.shape)
    spectrum = local_spectrum(normed_in, cosine, sine_table)
    kept_low = height_forward(to_modes(spectrum), real_table, imaginary_table).astype(jnp.bfloat16)
    shrunk, saved = spectral_forward(kept_low, spectral_in, spectral_bias, spectral_out)
    back = to_rows(height_inverse(shrunk, real_table, imaginary_table).astype(jnp.bfloat16))
    filtered = width_inverse(back, cosine_weighted, sine_weighted)
    output, grad_sum, grad_in, grad_out = token_block(
        field_now, normed_in, filtered, cot_now, project_in, project_out
    )
    output = back_to_cells(output)
    grad_spectrum = local_spectrum(grad_sum.astype(jnp.bfloat16), cosine_weighted, sine_weighted)
    grad_kept = height_forward(to_modes(grad_spectrum), real_table, imaginary_table)
    grad_modes, grad_first, grad_second, grad_bias = spectral_backward(
        grad_kept, kept_low, saved, spectral_in, spectral_out
    )
    grad_back = to_rows(
        height_inverse(grad_modes, real_table, imaginary_table).astype(jnp.bfloat16)
    )
    grad_filtered = width_inverse(grad_back, cosine, sine_table)
    grad_normed = grad_sum + grad_filtered.astype(jnp.float32)
    grad_flat = grad_sum.reshape(channels, -1) + norm_backward(
        normed_first, spread_first, grad_normed.reshape(channels, -1)
    )
    grad_weather = grad_flat.reshape(field_now.shape).astype(jnp.bfloat16)
    grad_weather = back_to_cells(grad_weather)
    grad_in, grad_out, grad_first, grad_second, grad_bias = lax.psum(
        (grad_in, grad_out, grad_first, grad_second, grad_bias), ("row", "col")
    )
    return (
        output,
        grad_weather,
        grad_in / H,
        grad_out / H,
        grad_first / H,
        grad_second / H,
        grad_bias / H,
    )


def solution(mesh):
    in_specs = (P(None, "row", "col"), P(None, "row", "col"), P(), P(), P(), P(), P())
    out_specs = (P(None, "row", "col"), P(None, "row", "col"), P(), P(), P(), P(), P())
    return jax.shard_map(body, mesh=mesh, in_specs=in_specs, out_specs=out_specs, check_vma=False)
```

profile of v0, /device:TPU:0, one launch (start us, length us, event | category | flops | bytes accessed | tf_op | source)
XLA Modules:
  0.0 2239.7 jit_solution(3339746357827792051)
XLA Ops:
  7.2 12.0 copy.154
  19.2 142.7 %all_to_all.132 = bf16[192,128,256]{2,0,1:T(8,128)(2,1)S(1)} all-to-all(bf16[192,128,256]{2,0,1:T(8,128)(2,1)S(1)} %copy.154), channel_id=1, replica_groups=mesh['row'=8,'col'=4] {'col'}, dimensions={1} | all-to-all | bytes 25165824 | tf_op jit(solution)/shard_map/all_to_all | solution.py:253
  165.0 32.4 %fusion.314 = f32[32,4,256]{2,1,0:T(4,128)S(1)} fusion(f32[192,4,32,256]{3,0,2,1:T(8,128)S(1)} %bitcast_convert_fusion.1), kind=kLoop, calls=%fused_computation.400 | loop fusion | flops 6258688 | bytes 25296896 | tf_op jit(solution)/shard_map/reduce_sum | solution.py:197
  197.5 31.0 %copy.339 = f32[192,4,32,256]{3,1,0,2:T(4,128)} copy(f32[192,4,32,256]{3,0,2,1:T(8,128)S(1)} %bitcast_convert_fusion.1) | data formatting | bytes 50331648 | tf_op jit(solution)/shard_map/convert_element_type | solution.py:212
  229.2 32.6 %multiply_reduce_fusion.2 = f32[32,4,256]{2,1,0:T(4,128)S(1)} fusion(f32[32,4,256]{2,1,0:T(4,128)S(1)} %get-tuple-element.33, f32[192,4,32,256]{3,0,2,1:T(8,128)S(1)} %bitcast_convert_fusion.1), kind=kLoop, calls=%fused_computation.54 | loop fusion | flops 18841600 | bytes 25427968 | tf_op jit(solution)/shard_map/reduce_sum | solution.py:198
  262.6 30.7 %reshape.210 = f32[192,32,1024]{2,0,1:T(8,128)} reshape(f32[192,32,4,256]{3,2,0,1:T(4,128)} %bitcast.564) | data formatting | bytes 50331648 | tf_op jit(solution)/shard_map/convert_element_type | solution.py:212
  293.2 14.6 convert_bitcast_fusion.2
  324.8 9.0 copy.157
  333.8 15.4 all-to-all-start.1
  349.2 14.0 copy.178
  363.2 127.2 %all-to-all-done.1 = bf16[32,256,384]{2,0,1:T(8,128)(2,1)} async-done(((bf16[32,256,384]{2,0,1:T(8,128)(2,1)}), bf16[32,256,384]{2,0,1:T(8,128)(2,1)}, u32[]{:S(2)}, u32[]{:S(2)}) %all-to-all-start.1) | async-done | bytes 6291488 | tf_op jit(solution)/shard_map/all_to_all | solution.py:241
  505.1 9.0 copy.160
  514.0 12.6 fusion.174
  526.7 11.8 fusion.182
  541.6 8.6 fusion.52
  550.8 8.7 fusion.49
  564.7 9.9 fusion.180
  574.7 13.2 fusion.172
  597.3 9.1 copy.171
  606.4 27.7 %all-to-all-done.4 = bf16[192,128,256]{2,0,1:T(8,128)(2,1)} async-done(((bf16[192,128,256]{2,0,1:T(8,128)(2,1)}), bf16[192,128,256]{2,0,1:T(8,128)(2,1)}, u32[]{:S(2)}, u32[]{:S(2)}) %all-to-all-start.4) | async-done | bytes 12582944 | tf_op jit(solution)/shard_map/all_to_all | solution.py:254
  639.0 17.1 copy.340
  656.2 20.9 reshape.206
  677.1 103.5 %all-to-all-done.2 = bf16[1024,8,384]{2,1,0:T(8,128)(2,1)} async-done(((bf16[1024,8,384]{2,1,0:T(8,128)(2,1)}), bf16[1024,8,384]{2,1,0:T(8,128)(2,1)}, u32[]{:S(2)}, u32[]{:S(2)}) %all-to-all-start.2) | async-done | bytes 6291488 | tf_op jit(solution)/shard_map/all_to_all | solution.py:245
  800.8 13.9 fusion.194
  814.7 12.2 fusion.195
  826.9 33.9 %fusion.316 = (f32[32,1024]{1,0:T(8,128)S(1)}, f32[192,32,1024]{2,0,1:T(8,128)}) fusion(f32[1024,32,192]{0,2,1:T(8,128)} %bitcast.567, f32[1024,32,192]{0,2,1:T(8,128)} %bitcast.568, f32[192,32,1024]{2,0,1:T(8,128)} %reshape.210, f32[32,1024]{1,0:T(8,128)S(1)} %bitcast.620, f32[32,1024]{1,0:T(8,128)S(1)} %bitcast.616), kind=kLoop, calls=%fused_computation.402 | loop fusion | flops 62881792 | bytes 101056512 | tf_op jit(solution)/shard_map/reduce_sum | solution.py:197
  860.9 10.4 multiply_reduce_fusion.1
  871.3 9.4 copy.260
  880.8 241.7 %fusion.2 = (bf16[768,32768]{0,1:T(8,128)(2,1)}, f32[32768,768]{1,0:T(8,128)}) fusion(bf16[192,768]{1,0:T(8,128)(2,1)S(1)} %copy-done, f32[192,32768]{1,0:T(8,128)S(1)} %bitcast.556, f32[32768]{0:T(1024)S(1)} %bitcast.609, f32[32768]{0:T(1024)S(1)} %bitcast.605), kind=kOutput, calls=%fused_computation.4 | convolution fusion | flops 11318329344 | bytes 176717824 | tf_op jit(solution)/shard_map/cn,ch->hn/dot_general | solution.py:21
  1122.5 50.7 %fusion.8 = bf16[768,32768]{0,1:T(8,128)(2,1)} fusion(f32[32768,768]{1,0:T(8,128)} %get-tuple-element.43, bf16[768,192]{0,1:T(8,128)(2,1)S(1)} %copy-done.43, bf16[192,32768]{1,0:T(8,128)(2,1)S(1)} %copy-done.4), kind=kOutput, calls=%fused_computation.10 | convolution fusion | flops 9915334656 | bytes 163872768 | tf_op jit(solution)/shard_map/cn,hc->hn/dot_general | solution.py:21
  1173.2 34.1 %fusion.28 = (f32[32768]{0:T(1024)S(1)}, f32[32768,192]{0,1:T(8,128)}) fusion(f32[192,32768]{1,0:T(8,128)} %bitcast.557, f32[32768]{0:T(1024)S(1)} %bitcast.610, f32[32768]{0:T(1024)S(1)} %bitcast.606, bf16[768,32768]{0,1:T(8,128)(2,1)} %fusion.8, bf16[192,768]{1,0:T(8,128)(2,1)S(1)} %copy-done), kind=kOutput, calls=%fused_computation.45 | convolution fusion | flops 9688809472 | bytes 101351424 | tf_op jit(solution)/shard_map/hn,ch->cn/dot_general | solution.py:21
  1207.3 10.0 reduce_sum.94
  1217.4 29.8 %fusion.27 = f32[192,32768]{1,0:T(8,128)} fusion(f32[32768,192]{0,1:T(8,128)} %get-tuple-element.45, bf16[192,32768]{1,0:T(8,128)(2,1)} %reshape.206, f32[192,32768]{1,0:T(8,128)} %bitcast.558, f32[32768]{0:T(1024)S(1)} %broadcast_multiply_fusion.4, f32[32768]{0:T(1024)S(1)} %broadcast_multiply_fusion.5, f32[32768]{0:T(1024)S(1)} %bitcast.611, ...), kind=kLoop, calls=%fused_computation.44 | loop fusion | flops 50331648 | bytes 88604672 | tf_op jit(solution)/shard_map/add | solution.py:226
  1247.2 24.6 %copy.268 = bf16[24,8,32,1024]{3,2,1,0:T(8,128)(2,1)} copy(f32[24,8,32,1024]{3,1,2,0:T(8,128)} %bitcast.561) | data formatting | bytes 37748736
  1271.8 22.5 %convert_bitcast_fusion = bf16[32,256,1,192]{1,3,0,2:T(8,128)(2,1)S(1)} fusion(bf16[192,32,1024]{2,1,0:T(8,128)(2,1)} %bitcast.589, f32[256]{0:T(256)S(1)} %copy-done.46), kind=kOutput, calls=%fused_computation.144 | convolution fusion | flops 3227254784 | bytes 15729664 | tf_op jit(solution)/shard_map/crw,wk->rkc/dot_general | solution.py:21
  1294.2 22.9 %convert_bitcast_fusion.1 = bf16[32,256,1,192]{1,3,0,2:T(8,128)(2,1)S(1)} fusion(bf16[192,32,1024]{2,1,0:T(8,128)(2,1)} %bitcast.590, f32[256]{0:T(256)S(1)} %copy-done.46), kind=kOutput, calls=%fused_computation.145 | convolution fusion | flops 3226992640 | bytes 15729664 | tf_op jit(solution)/shard_map/crw,wk->rkc/dot_general | solution.py:21
  1320.9 8.9 copy.184
  1329.7 144.2 %all_to_all.133 = bf16[32,256,384]{2,0,1:T(8,128)(2,1)S(1)} all-to-all(bf16[32,256,384]{2,0,1:T(8,128)(2,1)} %copy.184), channel_id=1, replica_groups=mesh['row'=8,'col'=4] {'row','col'}, dimensions={1} | all-to-all | bytes 12582912 | tf_op jit(solution)/shard_map/all_to_all | solution.py:241
  1479.5 9.0 copy.187
  1488.5 12.8 fusion.170
  1501.3 11.7 fusion.178
  1532.9 9.6 fusion.168
  1542.5 13.6 fusion.176
  1565.5 9.1 copy.200
  1578.2 30.2 %copy.338 = f32[192,4,32,256]{3,1,2,0:T(4,128)} copy(f32[192,4,32,256]{3,0,2,1:T(8,128)} %copy-done.1) | data formatting | bytes 50331648 | tf_op jit(solution)/shard_map/convert_element_type | solution.py:212
  1609.9 30.6 %reshape.211 = f32[192,32768]{1,0:T(8,128)} reshape(f32[192,32,4,256]{3,2,1,0:T(4,128)} %bitcast.565) | data formatting | bytes 50331648 | tf_op jit(solution)/shard_map/convert_element_type | solution.py:212
  1640.5 30.7 %fusion.24 = bf16[192,32768]{1,0:T(8,128)(2,1)} fusion(f32[192,32768]{1,0:T(8,128)} %bitcast.559, bf16[768,32768]{0,1:T(8,128)(2,1)} %get-tuple-element.42, bf16[768,192]{0,1:T(8,128)(2,1)S(1)} %copy-done.44), kind=kOutput, calls=%fused_computation.36 | convolution fusion | flops 9676259328 | bytes 88375296 | tf_op jit(solution)/shard_map/hn,hc->cn/dot_general | solution.py:21
  1671.2 14.5 copy.266
  1685.7 25.1 %copy.176 = bf16[192,32,1024]{0,1,2:T(8,128)(2,1)} copy(bf16[192,32,1024]{2,1,0:T(8,128)(2,1)} %bitcast.573) | data formatting | bytes 25165824 | tf_op jit(solution)/shard_map/reshape | solution.py:227
  1710.8 9.0 all-to-all-done.6
  1747.2 13.9 fusion.192
  1761.1 12.2 fusion.193
  1773.3 42.6 %fusion.315 = (f32[32,1024]{1,0:T(8,128)S(1)}, f32[32,1024]{1,0:T(8,128)S(1)}, f32[192,32,1024]{2,0,1:T(8,128)}) fusion(f32[32,1024]{1,0:T(8,128)S(1)} %bitcast.621, f32[192,32,1024]{2,0,1:T(8,128)} %reshape.210, f32[32,1024]{1,0:T(8,128)S(1)} %bitcast.617, f32[1024,32,192]{0,2,1:T(8,128)} %bitcast.570, f32[1024,32,192]{0,2,1:T(8,128)} %bitcast.571, ...), kind=kLoop, calls=%fused_computation.401 | loop fusion | flops 56557568 | bytes 126353408 | tf_op jit(solution)/shard_map/reduce_sum | solution.py:204
  1816.0 17.7 copy.261
  1833.7 24.0 %add_convert_fusion = bf16[192,32768]{1,0:T(8,128)(2,1)S(1)} fusion(f32[192,32768]{1,0:T(8,128)} %fusion.27, f32[192,32768]{1,0:T(8,128)} %reshape.211, f32[192,32768]{1,0:T(8,128)} %bitcast.566, f32[32768]{0:T(1024)S(1)} %bitcast.625, f32[32768]{0:T(1024)S(1)} %bitcast.622, f32[32768]{0:T(1024)S(1)} %bitcast.624, f32[32768]{0:T(1024)S(1)} %bitcast.623), kind=kLoop, calls=%fused_computation.48 | loop fusion | flops 50331648 | bytes 88604672 | tf_op jit(solution)/shard_map/convert_element_type | solution.py:280
  1857.7 8.6 copy.272
  1866.3 25.0 %copy.207 = bf16[192,32,1024]{0,1,2:T(8,128)(2,1)} copy(bf16[192,32,1024]{2,1,0:T(8,128)(2,1)} %bitcast.574) | data formatting | bytes 25165824 | tf_op jit(solution)/shard_map/convert_element_type | solution.py:280
  1891.4 18.0 all-to-all-done.3
  1916.5 23.7 %fusion.320 = f32[768,192]{0,1:T(8,128)} fusion(bf16[192,32768]{1,0:T(8,128)(2,1)} %reshape.206, bf16[768,32768]{0,1:T(8,128)(2,1)} %get-tuple-element.42), kind=kOutput, calls=%fused_computation.407 | convolution fusion | flops 9663676416 | bytes 63504384 | tf_op jit(solution)/shard_map/hn,cn->hc/dot_general | solution.py:21
  1940.1 27.3 %fusion.43 = f32[192,768]{1,0:T(8,128)} fusion(bf16[768,32768]{0,1:T(8,128)(2,1)} %fusion.8, f32[192,32768]{1,0:T(8,128)} %bitcast.560, f32[32768]{0:T(1024)} %bitcast.612, f32[32768]{0:T(1024)} %bitcast.608), kind=kOutput, calls=%fused_computation.84 | convolution fusion | flops 9682550784 | bytes 76349440 | tf_op jit(solution)/shard_map/cn,hn->ch/dot_general | solution.py:21
  1974.8 29.5 %copy.177 = bf16[192,4,32,256]{3,2,1,0:T(8,128)(2,1)} copy(bf16[192,4,32,256]{0,2,3,1:T(8,128)(2,1)} %bitcast.55) | data formatting | bytes 25165824 | tf_op jit(solution)/shard_map/all_to_all | solution.py:231
  2004.2 131.6 %psum.39 = f32[2,2,96]{2,1,0:T(2,128)S(1)} all-reduce(f32[2,2,96]{2,1,0:T(2,128)S(1)} %pad_maximum_fusion.9), channel_id=1, replica_groups=mesh['row'=8,'col'=4] {'row','col'}, use_global_device_ids=true, to_apply=%region_14.15 | all-reduce | flops 384 | bytes 3072 | tf_op jit(solution)/shard_map/psum | solution.py:282
  2136.4 59.5 %all-reduce.3.cloned.1.call-done = (f32[192,768]{1,0:T(8,128)}, f32[768,192]{0,1:T(8,128)}, f32[2,2,96,96]{3,2,1,0:T(8,128)}, f32[2,2,96,96]{3,2,1,0:T(8,128)}) async-done(((f32[192,768]{1,0:T(8,128)}, f32[768,192]{0,1:T(8,128)}, f32[2,2,96,96]{3,2,1,0:T(8,128)}, f32[2,2,96,96]{3,2,1,0:T(8,128)}), (f32[192,768]{1,0:T(8,128)}, f32[768,192]{0,1:T(8,128)}, f32[2,2,96,96]{3,2,1,0:T(8,128)}, ...) | async-done | bytes 1474576 | tf_op jit(solution)/shard_map/psum | solution.py:282
  2203.0 29.4 %copy.208 = bf16[192,4,32,256]{3,2,1,0:T(8,128)(2,1)} copy(bf16[192,4,32,256]{0,2,3,1:T(8,128)(2,1)} %bitcast.101) | data formatting | bytes 25165824 | tf_op jit(solution)/shard_map/all_to_all | solution.py:231
  (196 shorter events, 172.7 us)
Async XLA Ops:
  7.2 873.6 %copy-start = (bf16[192,768]{1,0:T(8,128)(2,1)S(1)}, bf16[192,768]{1,0:T(8,128)(2,1)}, u32[]{:S(2)}) copy-start(bf16[192,768]{1,0:T(8,128)(2,1)} %param.12) | copy-start | bytes 884740
  165.0 64.1 %copy-start.1 = (f32[192,4,32,256]{3,0,2,1:T(8,128)}, f32[192,4,32,256]{3,0,2,1:T(8,128)S(1)}, u32[]{:S(2)}) copy-start(f32[192,4,32,256]{3,0,2,1:T(8,128)S(1)} %bitcast_convert_fusion.1) | copy-start | bytes 75497472
  261.8 46.0 %copy-start.29 = (f32[4,8,4,256]{3,1,2,0:T(8,128)}, f32[4,8,4,256]{3,1,2,0:T(8,128)S(1)}, u32[]{:S(2)}) copy-start(f32[4,8,4,256]{3,1,2,0:T(8,128)S(1)} %copy.262) | copy-start | bytes 393220
  262.6 45.3 %copy-start.32 = (f32[4,8,4,256]{3,1,2,0:T(8,128)}, f32[4,8,4,256]{3,1,2,0:T(8,128)S(1)}, u32[]{:S(2)}) copy-start(f32[4,8,4,256]{3,1,2,0:T(8,128)S(1)} %copy.263) | copy-start | bytes 393220
  293.2 16.6 copy-start.3
  333.8 156.6 %all-to-all-start.1 = ((bf16[32,256,384]{2,0,1:T(8,128)(2,1)}), bf16[32,256,384]{2,0,1:T(8,128)(2,1)}, u32[]{:S(2)}, u32[]{:S(2)}) async-start(bf16[32,256,384]{2,0,1:T(8,128)(2,1)} %copy.157), calls=%async_computation.1 | async-start | bytes 12582912 | tf_op jit(solution)/shard_map/all_to_all | solution.py:241
  349.2 14.0 copy-start.47
  363.2 211.5 %copy-start.48 = (s32[512]{0:T(512)}, s32[512]{0:T(512)S(1)}, u32[]{:S(2)}) copy-start(s32[512]{0:T(512)S(1)} %compare_select_fusion) | copy-start | bytes 6148
  490.4 143.7 %all-to-all-start.4 = ((bf16[192,128,256]{2,0,1:T(8,128)(2,1)}), bf16[192,128,256]{2,0,1:T(8,128)(2,1)}, u32[]{:S(2)}, u32[]{:S(2)}) async-start(bf16[192,128,256]{2,0,1:T(8,128)(2,1)} %copy.178), calls=%async_computation.4 | async-start | bytes 25165824 | tf_op jit(solution)/shard_map/all_to_all | solution.py:254
  514.0 12.6 copy-start.17
  538.4 1.9 copy-start.37
  540.4 1.2 copy-start.25
  540.4 10.4 copy-start.23
  541.6 8.6 copy-start.35
  550.2 10.6 copy-start.9
  559.5 1.2 copy-start.11
  560.8 1.7 copy-start.7
  562.4 1.7 copy-start.5
  634.1 146.5 %all-to-all-start.2 = ((bf16[1024,8,384]{2,1,0:T(8,128)(2,1)}), bf16[1024,8,384]{2,1,0:T(8,128)(2,1)}, u32[]{:S(2)}, u32[]{:S(2)}) async-start(bf16[1024,8,384]{2,1,0:T(8,128)(2,1)} %copy.171), calls=%async_computation.2 | async-start | bytes 12582912 | tf_op jit(solution)/shard_map/all_to_all | solution.py:245
  639.0 175.7 %copy-start.45 = (f32[256]{0:T(256)}, f32[256]{0:T(256)S(1)}, u32[]{:S(2)}) copy-start(f32[256]{0:T(256)S(1)} %fusion.234) | copy-start | bytes 3076
  814.7 12.2 copy-start.30
  814.7 12.2 copy-start.33
  860.9 356.5 %copy-start.27 = (f32[4,8,8,128]{3,1,2,0:T(8,128)}, f32[4,8,8,128]{3,1,2,0:T(8,128)S(1)}, u32[]{:S(2)}) copy-start(f32[4,8,8,128]{3,1,2,0:T(8,128)S(1)} %copy.264) | copy-start | bytes 393220
  871.3 346.0 %copy-start.28 = (f32[4,8,8,128]{3,1,2,0:T(8,128)}, f32[4,8,8,128]{3,1,2,0:T(8,128)S(1)}, u32[]{:S(2)}) copy-start(f32[4,8,8,128]{3,1,2,0:T(8,128)S(1)} %copy.265) | copy-start | bytes 393220
  880.7 241.7 %copy-start.2 = (f32[32,24,8,1024]{3,2,0,1:T(8,128)}, f32[32,24,8,1024]{3,2,0,1:T(8,128)S(1)}, u32[]{:S(2)}) copy-start(f32[32,24,8,1024]{3,2,0,1:T(8,128)S(1)} %copy.260) | copy-start | bytes 75497472
  880.8 241.7 %copy-start.4 = (bf16[192,32768]{1,0:T(8,128)(2,1)S(1)}, bf16[192,32768]{1,0:T(8,128)(2,1)}, u32[]{:S(2)}) copy-start(bf16[192,32768]{1,0:T(8,128)(2,1)} %reshape.206) | copy-start | bytes 37748740
  880.8 241.7 %copy-start.43 = (bf16[768,192]{0,1:T(8,128)(2,1)S(1)}, bf16[768,192]{0,1:T(8,128)(2,1)}, u32[]{:S(2)}) copy-start(bf16[768,192]{0,1:T(8,128)(2,1)} %param.13) | copy-start | bytes 884740
  1247.2 24.6 %copy-start.46 = (f32[256]{0:T(256)S(1)}, f32[256]{0:T(256)}, u32[]{:S(2)}) copy-start(f32[256]{0:T(256)} %copy-done.45) | copy-start | bytes 3076
  1479.5 9.0 copy-start.49
  1488.5 12.8 copy-start.18
  1515.6 1.9 copy-start.8
  1517.5 2.1 copy-start.6
  1518.3 7.9 copy-start.13
  1519.6 0.9 copy-start.36
  1520.5 1.2 copy-start.15
  1521.0 1.9 copy-start.52
  1522.9 2.7 copy-start.38
  1525.6 6.1 copy-start.19
  1525.6 2.5 copy-start.53
  1530.6 1.1 copy-start.21
  1574.6 145.2 %all-to-all-start.6 = ((bf16[1024,8,384]{2,1,0:T(8,128)(2,1)}), bf16[1024,8,384]{2,1,0:T(8,128)(2,1)}, u32[]{:S(2)}, u32[]{:S(2)}) async-start(bf16[1024,8,384]{2,1,0:T(8,128)(2,1)} %copy.200), calls=%async_computation.6 | async-start | bytes 12582912 | tf_op jit(solution)/shard_map/all_to_all | solution.py:245
  1578.2 30.2 %copy-start.41 = (f32[32,2,4,128]{3,2,1,0:T(4,128)S(1)}, f32[32,2,4,128]{3,2,1,0:T(4,128)}, u32[]{:S(2)}) copy-start(f32[32,2,4,128]{3,2,1,0:T(4,128)} %get-tuple-element.32) | copy-start | bytes 393220
  1578.2 30.9 %copy-start.42 = (f32[32,2,4,128]{3,2,1,0:T(4,128)S(1)}, f32[32,2,4,128]{3,2,1,0:T(4,128)}, u32[]{:S(2)}) copy-start(f32[32,2,4,128]{3,2,1,0:T(4,128)} %get-tuple-element.30) | copy-start | bytes 393220
  1609.9 30.6 %copy-start.44 = (bf16[768,192]{0,1:T(8,128)(2,1)S(1)}, bf16[768,192]{0,1:T(8,128)(2,1)}, u32[]{:S(2)}) copy-start(bf16[768,192]{0,1:T(8,128)(2,1)} %param.13) | copy-start | bytes 884740
  1719.8 189.6 %all-to-all-start.3 = ((bf16[192,32,1024]{0,1,2:T(8,128)(2,1)}), bf16[192,32,1024]{0,1,2:T(8,128)(2,1)}, u32[]{:S(2)}, u32[]{:S(2)}) async-start(bf16[192,32,1024]{0,1,2:T(8,128)(2,1)} %copy.176), calls=%async_computation.3 | async-start | bytes 33554432 | tf_op jit(solution)/shard_map/all_to_all | solution.py:231
  1761.1 12.2 copy-start.31
  1761.1 12.2 copy-start.34
  1816.0 17.7 copy-start.39
  1816.0 17.7 copy-start.40
  1909.4 293.6 %all-to-all-start.7 = ((bf16[192,32,1024]{0,1,2:T(8,128)(2,1)}), bf16[192,32,1024]{0,1,2:T(8,128)(2,1)}, u32[]{:S(2)}, u32[]{:S(2)}) async-start(bf16[192,32,1024]{0,1,2:T(8,128)(2,1)} %copy.207), calls=%async_computation.7 | async-start | bytes 33554432 | tf_op jit(solution)/shard_map/all_to_all | solution.py:231
  1916.4 279.5 %all-reduce.3.cloned.1.call-start = ((), (), s32[]{:S(2)}) async-start(), calls=%async_computation.8 | async-start | bytes 3145728 | tf_op jit(solution)/shard_map/psum | solution.py:282
  1940.1 27.3 %copy-start.10 = (bf16[512,8,2,96]{0,3,1,2:T(8,128)(2,1)S(1)}, bf16[512,8,2,96]{0,3,1,2:T(8,128)(2,1)}, u32[]{:S(2)}) copy-start(bf16[512,8,2,96]{0,3,1,2:T(8,128)(2,1)} %copy-done.9) | copy-start | bytes 4718596
  1940.1 27.3 %copy-start.16 = (bf16[512,8,2,96]{0,3,1,2:T(8,128)(2,1)S(1)}, bf16[512,8,2,96]{0,3,1,2:T(8,128)(2,1)}, u32[]{:S(2)}) copy-start(bf16[512,8,2,96]{0,3,1,2:T(8,128)(2,1)} %copy-done.15) | copy-start | bytes 4718596
  1967.5 1.4 copy-start.14
  1967.5 2.0 copy-start.12
  1969.5 1.9 copy-start.22
  1969.5 1.9 copy-start.24
  1970.1 2.0 copy-start.26
  1971.4 1.5 copy-start.20
  1974.7 29.5 %copy-start.50 = (f32[2,96]{1,0:T(2,128)S(1)}, f32[2,96]{1,0:T(2,128)}, u32[]{:S(2)}) copy-start(f32[2,96]{1,0:T(2,128)} %get-tuple-element.46) | copy-start | bytes 2308
  1974.8 29.5 %copy-start.51 = (f32[2,96]{1,0:T(2,128)S(1)}, f32[2,96]{1,0:T(2,128)}, u32[]{:S(2)}) copy-start(f32[2,96]{1,0:T(2,128)} %get-tuple-element.48) | copy-start | bytes 2308
Sparse Core Ops, SparseCore 0:
  1974.9 221.0 all-reduce.2
where the time goes:
time: 2260 us; the launch traced here: 2240 us
  matrix products  658 us (29%)
  local copies, waits for them, and re-layouts  499 us (22%)
  blocking collectives  418 us (18%)
  waiting for transfers between devices  345 us (15%)
  other arithmetic  260 us (12%)
  starting transfers between devices  44.6 us (2%)
    dot_general x42, matrix products, product(): return jnp.einsum(form, left, right, preferred_element_type=jnp.float32)  606 us
    all_to_all x1, blocking collectives, to_modes(): lax.all_to_all(spectrum, ('row', 'col'), split_axis=1, concat_axis=0, til...  144 us
    all_to_all x1, blocking collectives, body(): lax.all_to_all(weather, 'col', split_axis=1, concat_axis=2, tiled=True)  143 us
    psum x1, blocking collectives, body(): lax.psum((grad_in, grad_out, grad_first, grad_second, grad_bias), ('row',...  132 us
    all_to_all x1, waiting for transfers between devices, to_modes(): lax.all_to_all(spectrum, ('row', 'col'), split_axis=1, concat_axis=0, til...  127 us
    convert_element_type x4, local copies, waits for them, and re-layouts, token_block(): weather.astype(jnp.float32) + normed_in.astype(jnp.float32)  122 us
    all_to_all x2, waiting for transfers between devices, to_rows(): lax.all_to_all(spectrum, ('row', 'col'), split_axis=0, concat_axis=1, til...  112 us
    unnamed x125, local copies, waits for them, and re-layouts  109 us
  transfers between devices with their start and end apart: 7, of which 6 were waited for; matrix products, arithmetic and copies ran while one was open for 25% of the time, Pallas kernels for 0%

commit v1 on v0

v1 whole, which is shorter than its diff:
```python
import functools
import math

import jax
import jax.numpy as jnp
import ml_dtypes
import numpy as np
from jax import lax
from jax.experimental import pallas as pl
from jax.experimental.pallas import tpu as pltpu
from jax.sharding import PartitionSpec as P

KH = 512
KW = 256

epsilon = 1e-05
threshold = 0.1
BF16 = jnp.bfloat16
F32 = jnp.float32
EVERY = ("row", "col")
VMEM_BYTES = 56 * 2**20
CHUNK_ROWS = 8
FIRST_US = 60
TOKEN_US = 100
LAST_US = 60
MODES_US = 60
RELAYOUT_US = 12


def width_tables(width, kept):
    position = np.arange(width, dtype=np.int32)
    frequency = np.arange(kept, dtype=np.int32)
    phases = position[:, None] * frequency[None, :] % width
    angles = phases.astype(np.float32) * np.float32(2.0 * math.pi / width)
    factor = np.float32(1.0 / math.sqrt(width))
    weight = np.where(frequency == 0, 1.0, 2.0).astype(np.float32)
    cosine = np.cos(angles) * factor
    sine_values = -np.sin(angles) * factor
    plain = np.concatenate([cosine, sine_values], axis=1)
    weighted = np.concatenate([cosine * weight[None, :], sine_values * weight[None, :]], axis=1)
    return plain.astype(ml_dtypes.bfloat16), weighted.astype(ml_dtypes.bfloat16)


def height_tables(height, kept):
    position = np.arange(height, dtype=np.int32)
    indices = np.arange(kept, dtype=np.int32)
    frequency = np.where(indices < kept // 2, indices, indices + (height - kept))
    phases = position[:, None] * frequency[None, :] % height
    angles = phases.astype(np.float32) * np.float32(2.0 * math.pi / height)
    factor = np.float32(1.0 / math.sqrt(height))
    both = np.concatenate([np.cos(angles) * factor, -np.sin(angles) * factor], axis=1)
    return both.astype(ml_dtypes.bfloat16)


def dot(left, right):
    return jnp.dot(left, right, preferred_element_type=F32)


def dot_rows(left, right):
    return lax.dot_general(left, right, (((1,), (1,)), ((), ())), preferred_element_type=F32)


def dot_columns(left, right):
    return lax.dot_general(left, right, (((0,), (0,)), ((), ())), preferred_element_type=F32)


def gelu_parts(values):
    share = 0.5 * (1.0 + lax.erf(values * (1.0 / math.sqrt(2.0))))
    density = jnp.exp(-0.5 * values * values) * (1.0 / math.sqrt(2.0 * math.pi))
    return share, share + values * density


def layer_norm(field):
    centred = field - jnp.mean(field, axis=0, keepdims=True)
    variance = jnp.mean(centred * centred, axis=0, keepdims=True)
    inverse_spread = lax.rsqrt(variance + epsilon)
    return centred * inverse_spread, inverse_spread


def norm_backward(normed, inverse_spread, gradient):
    mean_grad = jnp.mean(gradient, axis=0, keepdims=True)
    mean_cross = jnp.mean(gradient * normed, axis=0, keepdims=True)
    return inverse_spread * (gradient - mean_grad - normed * mean_cross)


def modes_first(spectrum):
    parts = jnp.concatenate([spectrum[:, :KW], spectrum[:, KW:]], axis=0)
    return parts.T.astype(BF16)


def channels_first(modes):
    turned = modes.astype(F32).T.astype(BF16)
    half = turned.shape[0] // 2
    return jnp.concatenate([turned[:half], turned[half:]], axis=1)


def first_kernel(count, order, *refs):
    fields, table, out = refs[:count], refs[count], refs[count + 1]
    total = None
    for slot in range(count):
        normed, _ = layer_norm(fields[slot][0].astype(F32))
        part = dot(normed.astype(BF16), table[order[slot]])
        total = part if total is None else total + part
    out[0] = modes_first(total)


def token_kernel(count, order, *refs):
    fields, cotangents = refs[:count], refs[count : 2 * count]
    back, inverse, forward, into, into_turned, onto, onto_turned = refs[2 * count : 2 * count + 7]
    outs = refs[2 * count + 7 : 3 * count + 7]
    kept_sum, spectrum, grad_onto, grad_into = refs[3 * count + 7 :]

    @pl.when(pl.program_id(0) == 0)
    def _():
        grad_onto[...] = jnp.zeros_like(grad_onto)
        grad_into[...] = jnp.zeros_like(grad_into)

    modes = channels_first(back[0])
    total = None
    for slot in range(count):
        field = fields[slot][0].astype(F32)
        normed_in = layer_norm(field)[0].astype(BF16)
        filtered = dot(modes, inverse[order[slot]]).astype(BF16)
        summed = field + normed_in.astype(F32) + filtered.astype(F32)
        normed, inverse_spread = layer_norm(summed)
        normed_low = normed.astype(BF16)
        cotangent = cotangents[slot][0]
        before = dot(into_turned[...], normed_low)
        back_hidden = dot(onto[...], cotangent)
        share, slope = gelu_parts(before)
        hidden = (before * share).astype(BF16)
        back_before = (back_hidden * slope).astype(BF16)
        outs[slot][0] = (summed + dot(onto_turned[...], hidden)).astype(BF16)
        grad_onto[...] += dot_rows(hidden, cotangent)
        grad_into[...] += dot_rows(back_before, normed_low)
        back_normed = dot(into[...], back_before)
        grad_sum = cotangent.astype(F32) + norm_backward(normed, inverse_spread, back_normed)
        kept_sum[0, slot] = grad_sum
        part = dot(grad_sum.astype(BF16), forward[order[slot]])
        total = part if total is None else total + part
    spectrum[0] = modes_first(total)


def last_kernel(count, order, *refs):
    fields, kept_sum, back, inverse = refs[:count], refs[count], refs[count + 1], refs[count + 2]
    outs = refs[count + 3 :]
    modes = channels_first(back[0])
    for slot in range(count):
        normed, inverse_spread = layer_norm(fields[slot][0].astype(F32))
        filtered = dot(modes, inverse[order[slot]]).astype(BF16)
        grad_sum = kept_sum[0, slot]
        grad_normed = grad_sum + filtered.astype(F32)
        outs[slot][0] = (grad_sum + norm_backward(normed, inverse_spread, grad_normed)).astype(BF16)


def swap_parts(values):
    lane = lax.broadcasted_iota(jnp.int32, values.shape, 1)
    half = values.shape[1] // 2
    turned = pltpu.roll(values, half, 1)
    return jnp.where(lane < half, -turned, turned)


def to_kept(pieces, table):
    rows = jnp.concatenate([piece[0] for piece in pieces], axis=0) if len(pieces) > 1 else pieces[0][0]
    both = dot(table[...], rows)
    return both[:KH] + swap_parts(both[KH:])


def from_kept(modes, table, outs):
    both = jnp.concatenate([modes.astype(BF16), (-swap_parts(modes)).astype(BF16)], axis=0)
    rows = dot(table[...], both).astype(BF16)
    size = rows.shape[0] // len(outs)
    for at, out in enumerate(outs):
        out[0] = rows[at * size : (at + 1) * size]


def modes_kernel(count, *refs):
    pieces = refs[:count]
    forward, inverse, weight_in, bias, weight_out = refs[count : count + 5]
    outs = refs[count + 5 : 2 * count + 5]
    kept_out, hidden_out, slope_out, shrink_out = refs[2 * count + 5 :]
    kept_low = to_kept(pieces, forward).astype(BF16)
    kept_out[0] = kept_low
    before = dot(kept_low, weight_in[...]) + bias[...]
    share, slope = gelu_parts(before)
    hidden = (before * share).astype(BF16)
    hidden_out[0] = hidden
    slope_out[0] = slope
    second = dot(hidden, weight_out[...])
    level = jnp.tanh(second * (1.0 / threshold))
    shrink_out[0] = level * level
    shrunk = second - threshold * level
    from_kept(shrunk, inverse, outs)


def modes_back_kernel(count, *refs):
    pieces = refs[:count]
    kept, hidden, slope, shrink = refs[count : count + 4]
    forward, inverse, weight_in, weight_out = refs[count + 4 : count + 8]
    outs = refs[count + 8 : 2 * count + 8]
    grad_in, grad_out, grad_bias = refs[2 * count + 8 :]

    @pl.when(pl.program_id(0) == 0)
    def _():
        grad_in[...] = jnp.zeros_like(grad_in)
        grad_out[...] = jnp.zeros_like(grad_out)
        grad_bias[...] = jnp.zeros_like(grad_bias)

    grad_second = (to_kept(pieces, forward) * shrink[0]).astype(BF16)
    grad_out[...] += dot_columns(hidden[0], grad_second)
    back_spec = dot_rows(grad_second, weight_out[...])
    gate = (back_spec * slope[0]).astype(BF16)
    grad_in[...] += dot_columns(kept[0], gate)
    grad_bias[...] += jnp.sum(gate.astype(F32), axis=0, keepdims=True)
    grad_modes = dot_rows(gate, weight_in[...])
    from_kept(grad_modes, inverse, outs)


def whole(array_shape):
    return pl.BlockSpec(array_shape, lambda *at: (0,) * len(array_shape))


def by_first(array_shape):
    rest = len(array_shape) - 1
    return pl.BlockSpec((1,) + tuple(array_shape[1:]), lambda at, *_: (at,) + (0,) * rest)


def params():
    return pltpu.CompilerParams(
        dimension_semantics=("arbitrary",), vmem_limit_bytes=VMEM_BYTES
    )


def weigh(microseconds):
    return pl.CostEstimate(
        flops=int(microseconds * 1.15e9), bytes_accessed=int(microseconds * 3.6e6), transcendentals=0
    )


def leave_out(kernel, start, count):
    def run(*refs):
        kernel(*refs[:start], *refs[start + count :])

    return run


def call_rows(kernel, weight, steps, order, stepped, fixed, step_outs, fixed_outs, waited=()):
    outs = list(step_outs) + list(fixed_outs)
    return pl.pallas_call(
        leave_out(kernel, 1 + len(stepped) + len(fixed), len(waited)),
        grid_spec=pltpu.PrefetchScalarGridSpec(
            num_scalar_prefetch=1,
            grid=(steps,),
            in_specs=[by_first(a.shape) for a in stepped]
            + [whole(a.shape) for a in fixed]
            + [pl.BlockSpec(memory_space=pl.ANY)] * len(waited),
            out_specs=[by_first(a.shape) for a in step_outs] + [whole(a.shape) for a in fixed_outs],
        ),
        out_shape=outs,
        compiler_params=params(),
        cost_estimate=weigh(weight),
    )(order, *stepped, *fixed, *waited)


def call_modes(kernel, weight, steps, stepped, fixed, step_outs, fixed_outs, waited=()):
    outs = list(step_outs) + list(fixed_outs)
    return pl.pallas_call(
        leave_out(kernel, len(stepped) + len(fixed), len(waited)),
        grid=(steps,),
        in_specs=[by_first(a.shape) for a in stepped]
        + [whole(a.shape) for a in fixed]
        + [pl.BlockSpec(memory_space=pl.ANY)] * len(waited),
        out_specs=[by_first(a.shape) for a in step_outs] + [whole(a.shape) for a in fixed_outs],
        out_shape=outs,
        compiler_params=params(),
        cost_estimate=weigh(weight),
    )(*stepped, *fixed, *waited)


def split_kernel(order, field, *outs):
    rows = jnp.swapaxes(field[:, 0], 0, 1)
    size = rows.shape[0] // len(outs)
    for at, out in enumerate(outs):
        out[0] = rows[at * size : (at + 1) * size]


def split_rows(field, order, own_rows, first, chunk, count):
    channels, local_rows, local_cols = field.shape
    groups, size = local_rows // own_rows, count * chunk
    return pl.pallas_call(
        split_kernel,
        grid_spec=pltpu.PrefetchScalarGridSpec(
            num_scalar_prefetch=1,
            grid=(groups,),
            in_specs=[
                pl.BlockSpec(
                    (channels, 1, size, local_cols), lambda at, order: (0, order[at], first // size, 0)
                )
            ],
            out_specs=[
                pl.BlockSpec((1, chunk, channels, local_cols), lambda at, order: (at, 0, 0, 0))
            ]
            * count,
        ),
        out_shape=[jax.ShapeDtypeStruct((groups, chunk, channels, local_cols), BF16)] * count,
        compiler_params=params(),
        cost_estimate=weigh(RELAYOUT_US),
    )(order, field.reshape(channels, groups, own_rows, local_cols))


def join_kernel(groups, count, order, *refs):
    pieces, out = refs[: groups * count], refs[-1]
    for slot in range(groups):

        @pl.when(pl.program_id(0) == slot)
        def _():
            rows = [pieces[at * groups + slot][...] for at in range(count)]
            out[...] = jnp.swapaxes(jnp.concatenate(rows, axis=0), 0, 1)


def join_rows(total, order, own_rows, first, per_chunk):
    groups, count = len(per_chunk[0]), len(per_chunk)
    chunk, channels, local_cols = per_chunk[0][0].shape
    size = count * chunk
    pieces = [piece for chunk_pieces in per_chunk for piece in chunk_pieces]
    given = [] if total is None else [total]
    return pl.pallas_call(
        functools.partial(join_kernel, groups, count),
        grid_spec=pltpu.PrefetchScalarGridSpec(
            num_scalar_prefetch=1,
            grid=(groups,),
            in_specs=[pl.BlockSpec(piece.shape, lambda at, order: (0, 0, 0)) for piece in pieces]
            + [pl.BlockSpec(memory_space=pl.ANY)] * len(given),
            out_specs=pl.BlockSpec(
                (channels, size, local_cols),
                lambda at, order: (0, order[at] * (own_rows // size) + first // size, 0),
            ),
        ),
        out_shape=jax.ShapeDtypeStruct((channels, groups * own_rows, local_cols), BF16),
        input_output_aliases={1 + len(pieces): 0} if given else {},
        compiler_params=params(),
        cost_estimate=weigh(RELAYOUT_US),
    )(order, *pieces, *given)


def scale_kernel(factor, *refs):
    count = len(refs) // 2
    for source, out in zip(refs[:count], refs[count:]):
        out[...] = source[...] * factor


def scale(arrays, factor, waited):
    return pl.pallas_call(
        leave_out(functools.partial(scale_kernel, factor), len(arrays), len(waited)),
        in_specs=[pl.BlockSpec(memory_space=pltpu.VMEM)] * len(arrays)
        + [pl.BlockSpec(memory_space=pl.ANY)] * len(waited),
        out_specs=[pl.BlockSpec(memory_space=pltpu.VMEM)] * len(arrays),
        out_shape=[jax.ShapeDtypeStruct(a.shape, a.dtype) for a in arrays],
        compiler_params=pltpu.CompilerParams(vmem_limit_bytes=VMEM_BYTES),
    )(*arrays, *waited)


def complex_matrix(weight):
    blocks, size = weight.shape[1], weight.shape[2]

    def diagonal(part):
        rows = []
        for at in range(blocks):
            rows.append(jnp.pad(part[at], ((0, 0), (at * size, (blocks - 1 - at) * size))))
        return jnp.concatenate(rows, axis=0)

    real, imaginary = diagonal(weight[0]), diagonal(weight[1])
    return jnp.concatenate(
        [
            jnp.concatenate([real, imaginary], axis=1),
            jnp.concatenate([-imaginary, real], axis=1),
        ],
        axis=0,
    )


def complex_gradient(total, blocks):
    half = total.shape[0] // 2
    size = half // blocks
    real = total[:half, :half] + total[half:, half:]
    imaginary = total[:half, half:] - total[half:, :half]

    def blocked(part):
        return jnp.stack(
            [
                part[at * size : (at + 1) * size, at * size : (at + 1) * size]
                for at in range(blocks)
            ]
        )

    return jnp.stack([blocked(real), blocked(imaginary)])


def body(
    row_count,
    col_count,
    weather,
    cotangent,
    spectral_in,
    spectral_bias,
    spectral_out,
    project_in,
    project_out,
):
    channels, local_rows, local_cols = weather.shape
    height, width = local_rows * row_count, local_cols * col_count
    devices = row_count * col_count
    own_rows = local_rows // col_count
    chunk = min(CHUNK_ROWS, own_rows)
    chunks = own_rows // chunk
    own_modes = KW // devices
    doubled = 2 * channels
    hidden_units = project_in.shape[1]
    blocks = spectral_in.shape[1]

    paired = col_count & (col_count - 1) == 0
    column = lax.axis_index("col")
    slots = jnp.arange(col_count, dtype=jnp.int32)
    target = column ^ slots if paired else (column + slots) % col_count
    origin = column ^ slots if paired else (column - slots) % col_count

    def partner(at, slot):
        return at ^ slot if paired else (at + slot) % col_count

    def send(piece, slot):
        if slot == 0:
            return piece
        return lax.ppermute(piece, "col", [(at, partner(at, slot)) for at in range(col_count)])

    def send_back(piece, slot):
        if slot == 0:
            return piece
        return lax.ppermute(piece, "col", [(partner(at, slot), at) for at in range(col_count)])

    def exchange(spectrum):
        return lax.all_to_all(spectrum, EVERY, split_axis=0, concat_axis=0, tiled=True)

    plain, weighted = width_tables(width, KW)
    forward_plain = jnp.asarray(plain.reshape(col_count, local_cols, 2 * KW))
    forward_weighted = jnp.asarray(weighted.reshape(col_count, local_cols, 2 * KW))
    inverse_plain = jnp.asarray(
        np.ascontiguousarray(plain.reshape(col_count, local_cols, 2 * KW).transpose(0, 2, 1))
    )
    inverse_weighted = jnp.asarray(
        np.ascontiguousarray(weighted.reshape(col_count, local_cols, 2 * KW).transpose(0, 2, 1))
    )
    row_order = np.arange(height).reshape(devices, chunks, chunk).transpose(1, 0, 2).reshape(-1)
    by_rows = height_tables(height, KH)[row_order]
    modes_inverse = jnp.asarray(by_rows)
    modes_forward = jnp.asarray(np.ascontiguousarray(by_rows.T))

    matrix_in, matrix_out = complex_matrix(spectral_in), complex_matrix(spectral_out)
    bias_row = spectral_bias.reshape(1, doubled)
    into_turned, onto_turned = project_in.T, project_out.T

    pair = 2 if chunks % 2 == 0 else 1

    def field_pieces(field, at):
        split = split_rows(field, target, own_rows, at * chunk, chunk, pair)
        return [[send(rows[slot], slot) for slot in range(col_count)] for rows in split]

    def to_modes(spectrum):
        parted = spectrum.reshape(chunk, devices, own_modes, doubled).transpose(1, 0, 2, 3)
        got = exchange(parted.reshape(devices, chunk * own_modes, doubled))
        got = got.reshape(devices * chunk, own_modes, doubled)
        return got.transpose(1, 0, 2)

    def to_rows(modes):
        parted = modes.reshape(own_modes, devices, chunk, doubled).transpose(1, 2, 0, 3)
        got = exchange(parted.reshape(devices, chunk * own_modes, doubled))
        got = got.reshape(devices, chunk, own_modes, doubled).transpose(1, 0, 2, 3)
        return got.reshape(chunk, KW, doubled)

    def place(total, pieces, at):
        for slot in range(col_count):
            total = lax.dynamic_update_slice(
                total, pieces[slot].transpose(1, 0, 2), (0, target[slot] * own_rows + at * chunk, 0)
            )
        return total

    def shape(*dims, kind=BF16):
        return jax.ShapeDtypeStruct(dims, kind)

    piece_shape = shape(chunk, channels, local_cols)
    spectrum_shape = shape(chunk, KW, doubled)
    rows_shape = shape(own_modes, devices * chunk, doubled)

    weather_now = sum([field_pieces(weather, at) for at in range(0, chunks, pair)], [])
    cot_now = sum([field_pieces(cotangent, at) for at in range(0, chunks, pair)], [])
    spectra = []
    for at in range(chunks):
        (spectrum,) = call_rows(
            functools.partial(first_kernel, col_count),
            FIRST_US,
            chunk,
            origin,
            weather_now[at],
            [forward_plain],
            [spectrum_shape],
            [],
        )
        spectra.append(to_modes(spectrum))

    mode_dims = (own_modes, KH, doubled)
    results = call_modes(
        functools.partial(modes_kernel, chunks),
            MODES_US,
        own_modes,
        spectra,
        [modes_forward, modes_inverse, matrix_in, bias_row, matrix_out],
        [rows_shape] * chunks
        + [shape(*mode_dims), shape(*mode_dims), shape(*mode_dims, kind=F32), shape(*mode_dims, kind=F32)],
        [],
        waited=[piece for pieces in cot_now[: chunks // 2] for piece in pieces],
    )
    back, saved = results[:chunks], results[chunks:]

    outputs, kept_sums, grad_spectra, grad_onto, grad_into = [], [], [], 0.0, 0.0
    for at in range(chunks):
        results = call_rows(
            functools.partial(token_kernel, col_count),
            TOKEN_US,
            chunk,
            origin,
            weather_now[at] + cot_now[at] + [to_rows(back[at])],
            [
                inverse_weighted,
                forward_weighted,
                project_in,
                into_turned,
                project_out,
                onto_turned,
            ],
            [piece_shape] * col_count
            + [shape(chunk, col_count, channels, local_cols, kind=F32), spectrum_shape],
            [shape(hidden_units, channels, kind=F32)] * 2,
        )
        spectrum = results[col_count + 1]
        outputs.append([send_back(results[slot], slot) for slot in range(col_count)])
        kept_sums.append(results[col_count])
        grad_spectra.append(to_modes(spectrum))
        grad_onto = grad_onto + results[col_count + 2]
        grad_into = grad_into + results[col_count + 3]
    early = chunks // 2
    results = call_modes(
        functools.partial(modes_back_kernel, chunks),
            MODES_US,
        own_modes,
        grad_spectra + list(saved),
        [modes_forward, modes_inverse, matrix_in, matrix_out],
        [rows_shape] * chunks,
        [
            shape(doubled, doubled, kind=F32),
            shape(doubled, doubled, kind=F32),
            shape(1, doubled, kind=F32),
        ],
        waited=[piece for pieces in outputs[:early] for piece in pieces],
    )
    grad_back = results[:chunks]
    grad_in_total, grad_out_total, grad_bias_total = results[chunks:]

    spectral_grads = jnp.stack(
        [complex_gradient(grad_in_total, blocks), complex_gradient(grad_out_total, blocks)]
    )
    packed = jnp.concatenate([spectral_grads.reshape(-1), grad_bias_total.reshape(-1)])
    token_grads, packed = lax.psum(
        (jnp.concatenate([grad_onto, grad_into], axis=0), packed.reshape(-1, 128)), EVERY
    )

    grads = []
    for at in range(chunks):
        results = call_rows(
            functools.partial(last_kernel, col_count),
            LAST_US,
            chunk,
            origin,
            weather_now[at] + [kept_sums[at], to_rows(grad_back[at])],
            [inverse_plain],
            [piece_shape] * col_count,
            [],
            waited=outputs[early + at // 2] if at % 2 == 0 and early + at // 2 < chunks else [],
        )
        grads.append([send_back(results[slot], slot) for slot in range(col_count)])
    token_grads, packed = scale([token_grads, packed], 1.0 / height, [results[0]])

    layer_out = None
    for at in range(0, chunks, pair):
        layer_out = join_rows(layer_out, target, own_rows, at * chunk, outputs[at : at + pair])
    grad_weather = join_rows(None, target, own_rows, 0, grads[:pair])
    for at in range(pair, chunks):
        grad_weather = place(grad_weather, grads[at], at)
    packed = packed.reshape(-1)
    spectral_grads = packed[:-doubled].reshape(spectral_grads.shape)
    return (
        layer_out,
        grad_weather,
        token_grads[hidden_units:].T,
        token_grads[:hidden_units],
        spectral_grads[0],
        spectral_grads[1],
        packed[-doubled:].reshape(spectral_bias.shape),
    )


def solution(mesh):
    in_specs = (P(None, "row", "col"), P(None, "row", "col"), P(), P(), P(), P(), P())
    out_specs = (P(None, "row", "col"), P(None, "row", "col"), P(), P(), P(), P(), P())
    run = functools.partial(body, mesh.shape["row"], mesh.shape["col"])
    return jax.shard_map(run, mesh=mesh, in_specs=in_specs, out_specs=out_specs, check_vma=False)
```

time: 2260 us -> 1180 us (0.52)
  matrix products: 658 us -> 0 us
  blocking collectives: 418 us -> 0 us
  local copies, waits for them, and re-layouts: 499 us -> 125 us
  Pallas kernels: 0 us -> 370 us
  other arithmetic: 260 us -> 6.47 us
  waiting for transfers between devices: 345 us -> 499 us
  starting transfers between devices: 44.6 us -> 157 us
    dot_general x42 -> x0, matrix products: 606 us -> none  [product(): return jnp.einsum(form, left, right, preferred_element_type=jnp.float32)]
    pallas_call x0 -> x22, Pallas kernels: none -> 370 us  [the longest x12 254 us: call_rows(): pl.pallas_call(leave_out(kernel, 1 + len(stepped) + len(fixed), len(waite...]
    all_to_all x2 -> x0, blocking collectives: 287 us -> none  [the longest x1 144 us: to_modes(): lax.all_to_all(spectrum, ('row', 'col'), split_axis=1, concat_axis=0, til...]
    ppermute x0 -> x48, waiting for transfers between devices: none -> 220 us  [the longest x24 130 us: send_back(): lax.ppermute(piece, 'col', [(partner(at, slot), at) for at in range(col_c...]
    convert_element_type x7 -> x0, local copies, waits for them, and re-layouts: 165 us -> none  [the longest x4 122 us: token_block(): weather.astype(jnp.float32) + normed_in.astype(jnp.float32)]
    reduce_sum x6 -> x0, other arithmetic: 162 us -> none  [the longest x2 66.4 us: layer_norm(): centred = flat_field - jnp.mean(flat_field, axis=0, keepdims=True)]
    psum x1 -> x0, blocking collectives: 132 us -> none  [body(): lax.psum((grad_in, grad_out, grad_first, grad_second, grad_bias), ('row',...]
    all_to_all x9 -> x0, local copies, waits for them, and re-layouts: 116 us -> none  [the longest x2 58.9 us: back_to_cells(): lax.all_to_all(field_part, 'col', split_axis=2, concat_axis=1, tiled=True)]
  transfers between devices with their start and end apart: 7 -> 65, of which waited for: 6 -> 31; matrix products, arithmetic and copies ran while one was open for 25% -> 10% of each run, Pallas kernels for 0% -> 28%
where the time goes in v1:
time: 1180 us
  waiting for transfers between devices  499 us (42%)
  Pallas kernels  370 us (31%)
  starting transfers between devices  157 us (13%)
  local copies, waits for them, and re-layouts  125 us (11%)
  between operations  17.5 us (1%)
    all_to_all x16, waiting for transfers between devices, exchange(): lax.all_to_all(spectrum, EVERY, split_axis=0, concat_axis=0, tiled=True)  259 us
    pallas_call x12, Pallas kernels, call_rows(): pl.pallas_call(leave_out(kernel, 1 + len(stepped) + len(fixed), len(waite...  254 us
    ppermute x24, waiting for transfers between devices, send_back(): lax.ppermute(piece, 'col', [(partner(at, slot), at) for at in range(col_c...  130 us
    all_to_all x16, starting transfers between devices, exchange(): lax.all_to_all(spectrum, EVERY, split_axis=0, concat_axis=0, tiled=True)  89.8 us
    ppermute x24, waiting for transfers between devices, send(): lax.ppermute(piece, 'col', [(at, partner(at, slot)) for at in range(col_c...  89.5 us
    pallas_call x2, Pallas kernels, call_modes(): pl.pallas_call(leave_out(kernel, len(stepped) + len(fixed), len(waited)),...  64.6 us
    ppermute x24, starting transfers between devices, send(): lax.ppermute(piece, 'col', [(at, partner(at, slot)) for at in range(col_c...  34.5 us
    ppermute x24, starting transfers between devices, send_back(): lax.ppermute(piece, 'col', [(partner(at, slot), at) for at in range(col_c...  32.2 us
  transfers between devices with their start and end apart: 65, of which 31 were waited for; matrix products, arithmetic and copies ran while one was open for 10% of the time, Pallas kernels for 28%

profile of v1, /device:TPU:0, one launch (start us, length us, event | category | flops | bytes accessed | tf_op | source)
XLA Modules:
  0.0 1175.1 jit_solution(469398066842114943)
XLA Ops:
  7.7 6.8 shard_map.182
  27.1 6.8 shard_map.180
  42.0 14.9 %collective-permute-done.7.refs_3_ = bf16[8,192,256]{2,1,0:T(8,128)(2,1)S(1)} collective-permute-done((bf16[8,192,256]{2,1,0:T(8,128)(2,1)S(1)}, bf16[8,192,256]{2,1,0:T(8,128)(2,1)S(1)}, u32[]{:S(2)}, u32[]{:S(2)}) %collective-permute-start.7) | collective-permute-done | bytes 786464 | tf_op jit(solution)/shard_map/ppermute | solution.py:433
  60.8 9.2 shard_map.183
  72.8 19.2 %all-to-all-start = ((bf16[32,64,384]{2,1,0:T(8,128)(2,1)}), bf16[32,64,384]{2,1,0:T(8,128)(2,1)S(1)}, u32[]{:S(2)}, u32[]{:S(2)}) async-start(bf16[32,64,384]{2,1,0:T(8,128)(2,1)} %copy_bitcast_fusion.31), calls=%async_computation | async-start | bytes 3145728 | tf_op jit(solution)/shard_map/all_to_all | solution.py:441
  95.6 9.2 shard_map.184
  107.6 12.5 %collective-permute-done.2.refs_4_ = bf16[8,192,256]{2,1,0:T(8,128)(2,1)} collective-permute-done((bf16[8,192,256]{2,1,0:T(8,128)(2,1)S(1)}, bf16[8,192,256]{2,1,0:T(8,128)(2,1)}, u32[]{:S(2)}, u32[]{:S(2)}) %collective-permute-start.2) | collective-permute-done | bytes 786464 | tf_op jit(solution)/shard_map/ppermute | solution.py:433
  121.3 18.8 %all-to-all-done = bf16[32,64,384]{2,1,0:T(8,128)(2,1)S(1)} async-done(((bf16[32,64,384]{2,1,0:T(8,128)(2,1)}), bf16[32,64,384]{2,1,0:T(8,128)(2,1)S(1)}, u32[]{:S(2)}, u32[]{:S(2)}) %all-to-all-start) | async-done | bytes 1572896 | tf_op jit(solution)/shard_map/all_to_all | solution.py:441
  141.3 6.3 all-to-all-start.1
  147.6 9.2 shard_map.185
  159.6 34.2 %all-to-all-done.1 = bf16[32,64,384]{2,1,0:T(8,128)(2,1)S(1)} async-done(((bf16[32,64,384]{2,1,0:T(8,128)(2,1)}), bf16[32,64,384]{2,1,0:T(8,128)(2,1)S(1)}, u32[]{:S(2)}, u32[]{:S(2)}) %all-to-all-start.1) | async-done | bytes 1572896 | tf_op jit(solution)/shard_map/all_to_all | solution.py:441
  193.9 6.9 all-to-all-start.2
  200.8 9.2 shard_map.186
  212.9 25.4 %all-to-all-done.2 = bf16[32,64,384]{2,1,0:T(8,128)(2,1)S(1)} async-done(((bf16[32,64,384]{2,1,0:T(8,128)(2,1)}), bf16[32,64,384]{2,1,0:T(8,128)(2,1)S(1)}, u32[]{:S(2)}, u32[]{:S(2)}) %all-to-all-start.2) | async-done | bytes 1572896 | tf_op jit(solution)/shard_map/all_to_all | solution.py:441
  238.3 4.5 all-to-all-start.3
  242.8 6.8 shard_map.187
  262.6 21.4 %collective-permute-done.17.refs_12_.refs_8_ = bf16[8,192,256]{2,1,0:T(8,128)(2,1)} collective-permute-done((bf16[8,192,256]{2,1,0:T(8,128)(2,1)}, bf16[8,192,256]{2,1,0:T(8,128)(2,1)}, u32[]{:S(2)}, u32[]{:S(2)}) %collective-permute-start.17) | collective-permute-done | bytes 786464 | tf_op jit(solution)/shard_map/ppermute | solution.py:433
  293.9 4.9 collective-permute-done.16.refs_11_.refs_7_
  300.5 17.3 %collective-permute-done.20.refs_16_.refs_8_ = bf16[8,192,256]{2,1,0:T(8,128)(2,1)} collective-permute-done((bf16[8,192,256]{2,1,0:T(8,128)(2,1)}, bf16[8,192,256]{2,1,0:T(8,128)(2,1)}, u32[]{:S(2)}, u32[]{:S(2)}) %collective-permute-start.20) | collective-permute-done | bytes 786464 | tf_op jit(solution)/shard_map/ppermute | solution.py:433
  317.8 14.7 %collective-permute-done.19.refs_15_.refs_7_ = bf16[8,192,256]{2,1,0:T(8,128)(2,1)} collective-permute-done((bf16[8,192,256]{2,1,0:T(8,128)(2,1)}, bf16[8,192,256]{2,1,0:T(8,128)(2,1)}, u32[]{:S(2)}, u32[]{:S(2)}) %collective-permute-start.19) | collective-permute-done | bytes 786464 | tf_op jit(solution)/shard_map/ppermute | solution.py:433
  333.7 31.2 %shard_map.188 = (bf16[8,256,384]{2,1,0:T(8,128)(2,1)}, bf16[8,256,384]{2,1,0:T(8,128)(2,1)}, bf16[8,256,384]{2,1,0:T(8,128)(2,1)}, bf16[8,256,384]{2,1,0:T(8,12...) custom-call(bf16[8,256,384]{2,1,0:T(8,128)(2,1)} %bitcast.348, ...), custom_call_target="tpu_custom_call" | custom-call | flops 69000003584 | bytes 216000000 | tf_op jit(solution)/shard_map/pallas_call | solution.py:267
  364.9 4.0 copy.133
  368.9 4.3 all-to-all-start.5
  375.9 34.9 %all-to-all-done.5 = bf16[32,64,384]{2,1,0:T(8,128)(2,1)S(1)} async-done(((bf16[32,64,384]{2,1,0:T(8,128)(2,1)}), bf16[32,64,384]{2,1,0:T(8,128)(2,1)S(1)}, u32[]{:S(2)}, u32[]{:S(2)}) %all-to-all-start.5) | async-done | bytes 1572896 | tf_op jit(solution)/shard_map/all_to_all | solution.py:441
  411.9 4.1 all-to-all-start.7
  416.0 4.1 copy.132
  420.1 33.4 %all-to-all-done.7 = bf16[32,64,384]{2,1,0:T(8,128)(2,1)S(1)} async-done(((bf16[32,64,384]{2,1,0:T(8,128)(2,1)}), bf16[32,64,384]{2,1,0:T(8,128)(2,1)S(1)}, u32[]{:S(2)}, u32[]{:S(2)}) %all-to-all-start.7) | async-done | bytes 1572896 | tf_op jit(solution)/shard_map/all_to_all | solution.py:441
  453.5 4.6 all-to-all-start.6
  458.1 6.8 shard_map.181
  480.1 4.0 copy.134
  485.4 10.3 all-to-all-done.6
  495.7 4.1 all-to-all-start.4
  499.8 42.8 %shard_map.192 = (bf16[8,192,256]{2,1,0:T(8,128)(2,1)}, bf16[8,192,256]{2,1,0:T(8,128)(2,1)}, bf16[8,192,256]{2,1,0:T(8,128)(2,1)}, bf16[8,192,256]{2,1,0:T(8,12...) custom-call(s32[4]{0:T(128)} %iota_xor_fusion.order.refs_0_, ...), custom_call_target="tpu_custom_call" | custom-call | flops 115000000512 | bytes 360000000 | tf_op jit(solution)/shard_map/pallas_call | solution.py:249
  546.8 17.7 %all-to-all-done.4 = bf16[32,64,384]{2,1,0:T(8,128)(2,1)S(1)} async-done(((bf16[32,64,384]{2,1,0:T(8,128)(2,1)}), bf16[32,64,384]{2,1,0:T(8,128)(2,1)S(1)}, u32[]{:S(2)}, u32[]{:S(2)}) %all-to-all-start.4) | async-done | bytes 1572896 | tf_op jit(solution)/shard_map/all_to_all | solution.py:441
  569.4 42.8 %shard_map.191 = (bf16[8,192,256]{2,1,0:T(8,128)(2,1)}, bf16[8,192,256]{2,1,0:T(8,128)(2,1)}, bf16[8,192,256]{2,1,0:T(8,128)(2,1)}, bf16[8,192,256]{2,1,0:T(8,12...) custom-call(s32[4]{0:T(128)} %iota_xor_fusion.order.refs_0_, ...), custom_call_target="tpu_custom_call" | custom-call | flops 115000000512 | bytes 360000000 | tf_op jit(solution)/shard_map/pallas_call | solution.py:249
  619.6 4.6 all-to-all-start.8
  624.3 42.8 %shard_map.189 = (bf16[8,192,256]{2,1,0:T(8,128)(2,1)}, bf16[8,192,256]{2,1,0:T(8,128)(2,1)}, bf16[8,192,256]{2,1,0:T(8,128)(2,1)}, bf16[8,192,256]{2,1,0:T(8,12...) custom-call(s32[4]{0:T(128)} %iota_xor_fusion.order.refs_0_, ...), custom_call_target="tpu_custom_call" | custom-call | flops 115000000512 | bytes 360000000 | tf_op jit(solution)/shard_map/pallas_call | solution.py:249
  671.4 6.0 all-to-all-start.10
  677.5 42.8 %shard_map.190 = (bf16[8,192,256]{2,1,0:T(8,128)(2,1)}, bf16[8,192,256]{2,1,0:T(8,128)(2,1)}, bf16[8,192,256]{2,1,0:T(8,128)(2,1)}, bf16[8,192,256]{2,1,0:T(8,12...) custom-call(s32[4]{0:T(128)} %iota_xor_fusion.order.refs_0_, ...), custom_call_target="tpu_custom_call" | custom-call | flops 115000000512 | bytes 360000000 | tf_op jit(solution)/shard_map/pallas_call | solution.py:249
  723.1 6.1 all-to-all-start.11
  739.2 26.5 %collective-permute-done.33.refs_5_.refs_17_ = bf16[8,192,256]{2,1,0:T(8,128)(2,1)} collective-permute-done((bf16[8,192,256]{2,1,0:T(8,128)(2,1)}, bf16[8,192,256]{2,1,0:T(8,128)(2,1)}, u32[]{:S(2)}, u32[]{:S(2)}) %collective-permute-start.33) | collective-permute-done | bytes 786464 | tf_op jit(solution)/shard_map/ppermute | solution.py:438
  773.4 10.5 collective-permute-done.35.refs_7_.refs_19_
  784.5 15.4 %collective-permute-done.30.refs_1_.refs_13_ = bf16[8,192,256]{2,1,0:T(8,128)(2,1)S(1)} collective-permute-done((bf16[8,192,256]{2,1,0:T(8,128)(2,1)}, bf16[8,192,256]{2,1,0:T(8,128)(2,1)S(1)}, u32[]{:S(2)}, u32[]{:S(2)}) %collective-permute-start.30) | collective-permute-done | bytes 786464 | tf_op jit(solution)/shard_map/ppermute | solution.py:438
  802.7 14.9 %collective-permute-done.32.refs_3_.refs_15_ = bf16[8,192,256]{2,1,0:T(8,128)(2,1)S(1)} collective-permute-done((bf16[8,192,256]{2,1,0:T(8,128)(2,1)}, bf16[8,192,256]{2,1,0:T(8,128)(2,1)S(1)}, u32[]{:S(2)}, u32[]{:S(2)}) %collective-permute-start.32) | collective-permute-done | bytes 786464 | tf_op jit(solution)/shard_map/ppermute | solution.py:438
  818.5 7.2 shard_map.193.refs_8_
  835.8 33.4 %shard_map.195 = (bf16[8,256,384]{2,1,0:T(8,128)(2,1)}, bf16[8,256,384]{2,1,0:T(8,128)(2,1)}, bf16[8,256,384]{2,1,0:T(8,128)(2,1)}, bf16[8,256,384]{2,1,0:T(8,12...) custom-call(bf16[8,256,384]{2,1,0:T(8,128)(2,1)} %bitcast.351, bf16[8,256,384]{2,1,0:T(8,128)(2,1)} %bitcast.349, ...), custom_call_target="tpu_custom_call" | custom-call | flops 69000003584 | bytes 216000000 | tf_op jit(solution)/shard_map/pallas_call | solution.py:267
  869.2 4.0 copy.126
  877.7 13.0 %collective-permute-done.29.refs_7_.refs_11_ = bf16[8,192,256]{2,1,0:T(8,128)(2,1)S(1)} collective-permute-done((bf16[8,192,256]{2,1,0:T(8,128)(2,1)S(1)}, bf16[8,192,256]{2,1,0:T(8,128)(2,1)S(1)}, u32[]{:S(2)}, u32[]{:S(2)}) %collective-permute-start.29) | collective-permute-done | bytes 786464 | tf_op jit(solution)/shard_map/ppermute | solution.py:438
  891.6 7.2 shard_map.194
  910.1 4.6 all-to-all-done.12
  914.7 4.2 all-to-all-start.13
  920.2 11.4 shard_map.196
  935.2 29.7 %all-to-all-done.13 = bf16[32,64,384]{2,1,0:T(8,128)(2,1)S(1)} async-done(((bf16[32,64,384]{2,1,0:T(8,128)(2,1)}), bf16[32,64,384]{2,1,0:T(8,128)(2,1)S(1)}, u32[]{:S(2)}, u32[]{:S(2)}) %all-to-all-start.13) | async-done | bytes 1572896 | tf_op jit(solution)/shard_map/all_to_all | solution.py:441
  969.5 11.4 shard_map.197
  984.2 23.2 %all-to-all-done.14 = bf16[32,64,384]{2,1,0:T(8,128)(2,1)S(1)} async-done(((bf16[32,64,384]{2,1,0:T(8,128)(2,1)}), bf16[32,64,384]{2,1,0:T(8,128)(2,1)S(1)}, u32[]{:S(2)}, u32[]{:S(2)}) %all-to-all-start.14) | async-done | bytes 1572896 | tf_op jit(solution)/shard_map/all_to_all | solution.py:441
  1012.4 11.4 shard_map.199
  1023.8 27.1 %all-to-all-done.15 = bf16[32,64,384]{2,1,0:T(8,128)(2,1)S(1)} async-done(((bf16[32,64,384]{2,1,0:T(8,128)(2,1)}), bf16[32,64,384]{2,1,0:T(8,128)(2,1)S(1)}, u32[]{:S(2)}, u32[]{:S(2)}) %all-to-all-start.15) | async-done | bytes 1572896 | tf_op jit(solution)/shard_map/all_to_all | solution.py:441
  1054.8 11.5 shard_map.200
  1066.3 20.1 %all-reduce.11.cloned.1.call-done = (f32[1536,192]{1,0:T(8,128)}, f32[579,128]{1,0:T(8,128)}) async-done(((f32[1536,192]{1,0:T(8,128)}, f32[579,128]{1,0:T(8,128)}), (f32[1536,192]{1,0:T(8,128)}, f32[579,128]{1,0:T(8,128)})) %all-reduce.11.cloned.1.call-update) | async-done | bytes 1476112 | tf_op jit(solution)/shard_map/psum | solution.py:571
  1100.3 7.2 shard_map.198
  1108.8 6.9 collective-permute-done.42
  1118.3 15.3 %collective-permute-done.43 = bf16[8,192,256]{2,1,0:T(8,128)(2,1)S(1)} collective-permute-done((bf16[8,192,256]{2,1,0:T(8,128)(2,1)S(1)}, bf16[8,192,256]{2,1,0:T(8,128)(2,1)S(1)}, u32[]{:S(2)}, u32[]{:S(2)}) %collective-permute-start.43) | collective-permute-done | bytes 786464 | tf_op jit(solution)/shard_map/ppermute | solution.py:438
  1137.5 12.0 %collective-permute-done.45 = bf16[8,192,256]{2,1,0:T(8,128)(2,1)S(1)} collective-permute-done((bf16[8,192,256]{2,1,0:T(8,128)(2,1)}, bf16[8,192,256]{2,1,0:T(8,128)(2,1)S(1)}, u32[]{:S(2)}, u32[]{:S(2)}) %collective-permute-start.45) | collective-permute-done | bytes 786464 | tf_op jit(solution)/shard_map/ppermute | solution.py:438
  1150.8 14.6 %collective-permute-done.46 = bf16[8,192,256]{2,1,0:T(8,128)(2,1)S(1)} collective-permute-done((bf16[8,192,256]{2,1,0:T(8,128)(2,1)}, bf16[8,192,256]{2,1,0:T(8,128)(2,1)S(1)}, u32[]{:S(2)}, u32[]{:S(2)}) %collective-permute-start.46) | collective-permute-done | bytes 786464 | tf_op jit(solution)/shard_map/ppermute | solution.py:438
  (276 shorter events, 205.3 us)
Async XLA Ops:
  17.7 22.3 %collective-permute-start.8 = (bf16[8,192,256]{2,1,0:T(8,128)(2,1)S(1)}, bf16[8,192,256]{2,1,0:T(8,128)(2,1)S(1)}, u32[]{:S(2)}, u32[]{:S(2)}) collective-permute-start(bf16[8,192,256]{2,1,0:T(8,128)(2,1)S(1)} %get-tuple-element.189), channel_id=1, source_target_pairs={{0,3},{1,2},{2,1},{3,0},{4,7},{5,6},{6,5},{7,4},{8,11},{9,10},{10,... | collective-permute-start | bytes 2359304 | tf_op jit(solution)/shard_map/ppermute | solution.py:433
  21.6 35.3 %collective-permute-start.7 = (bf16[8,192,256]{2,1,0:T(8,128)(2,1)S(1)}, bf16[8,192,256]{2,1,0:T(8,128)(2,1)S(1)}, u32[]{:S(2)}, u32[]{:S(2)}) collective-permute-start(bf16[8,192,256]{2,1,0:T(8,128)(2,1)S(1)} %get-tuple-element.190), channel_id=1, source_target_pairs={{0,2},{1,3},{2,0},{3,1},{4,6},{5,7},{6,4},{7,5},{8,10},{9,11},{10,... | collective-permute-start | bytes 2359304 | tf_op jit(solution)/shard_map/ppermute | solution.py:433
  22.1 37.8 %collective-permute-start.6 = (bf16[8,192,256]{2,1,0:T(8,128)(2,1)S(1)}, bf16[8,192,256]{2,1,0:T(8,128)(2,1)S(1)}, u32[]{:S(2)}, u32[]{:S(2)}) collective-permute-start(bf16[8,192,256]{2,1,0:T(8,128)(2,1)S(1)} %get-tuple-element.191), channel_id=1, source_target_pairs={{0,1},{1,0},{2,3},{3,2},{4,5},{5,4},{6,7},{7,6},{8,9},{9,8},{10,11... | collective-permute-start | bytes 2359304 | tf_op jit(solution)/shard_map/ppermute | solution.py:433
  23.7 68.3 %collective-permute-start.11 = (bf16[8,192,256]{2,1,0:T(8,128)(2,1)}, bf16[8,192,256]{2,1,0:T(8,128)(2,1)}, u32[]{:S(2)}, u32[]{:S(2)}) collective-permute-start(bf16[8,192,256]{2,1,0:T(8,128)(2,1)} %get-tuple-element.185), channel_id=1, source_target_pairs={{0,3},{1,2},{2,1},{3,0},{4,7},{5,6},{6,5},{7,4},{8,11},{9,10},{10,... | collective-permute-start | bytes 2359304 | tf_op jit(solution)/shard_map/ppermute | solution.py:433
  26.6 67.2 %collective-permute-start.10 = (bf16[8,192,256]{2,1,0:T(8,128)(2,1)}, bf16[8,192,256]{2,1,0:T(8,128)(2,1)}, u32[]{:S(2)}, u32[]{:S(2)}) collective-permute-start(bf16[8,192,256]{2,1,0:T(8,128)(2,1)} %get-tuple-element.186), channel_id=1, source_target_pairs={{0,2},{1,3},{2,0},{3,1},{4,6},{5,7},{6,4},{7,5},{8,10},{9,11},{10,... | collective-permute-start | bytes 2359304 | tf_op jit(solution)/shard_map/ppermute | solution.py:433
  40.0 55.3 %collective-permute-start.9 = (bf16[8,192,256]{2,1,0:T(8,128)(2,1)S(1)}, bf16[8,192,256]{2,1,0:T(8,128)(2,1)}, u32[]{:S(2)}, u32[]{:S(2)}) collective-permute-start(bf16[8,192,256]{2,1,0:T(8,128)(2,1)S(1)} %get-tuple-element.187), channel_id=1, source_target_pairs={{0,1},{1,0},{2,3},{3,2},{4,5},{5,4},{6,7},{7,6},{8,9},{9,8},{10,11... | collective-permute-start | bytes 2359304 | tf_op jit(solution)/shard_map/ppermute | solution.py:433
  56.9 63.1 %collective-permute-start.2 = (bf16[8,192,256]{2,1,0:T(8,128)(2,1)S(1)}, bf16[8,192,256]{2,1,0:T(8,128)(2,1)}, u32[]{:S(2)}, u32[]{:S(2)}) collective-permute-start(bf16[8,192,256]{2,1,0:T(8,128)(2,1)S(1)} %get-tuple-element.197), channel_id=1, source_target_pairs={{0,3},{1,2},{2,1},{3,0},{4,7},{5,6},{6,5},{7,4},{8,11},{9,10},{10,... | collective-permute-start | bytes 2359304 | tf_op jit(solution)/shard_map/ppermute | solution.py:433
  59.9 87.7 %collective-permute-start.1 = (bf16[8,192,256]{2,1,0:T(8,128)(2,1)}, bf16[8,192,256]{2,1,0:T(8,128)(2,1)}, u32[]{:S(2)}, u32[]{:S(2)}) collective-permute-start(bf16[8,192,256]{2,1,0:T(8,128)(2,1)} %get-tuple-element.198), channel_id=1, source_target_pairs={{0,2},{1,3},{2,0},{3,1},{4,6},{5,7},{6,4},{7,5},{8,10},{9,11},{10,... | collective-permute-start | bytes 2359304 | tf_op jit(solution)/shard_map/ppermute | solution.py:433
  72.8 67.4 %all-to-all-start = ((bf16[32,64,384]{2,1,0:T(8,128)(2,1)}), bf16[32,64,384]{2,1,0:T(8,128)(2,1)S(1)}, u32[]{:S(2)}, u32[]{:S(2)}) async-start(bf16[32,64,384]{2,1,0:T(8,128)(2,1)} %copy_bitcast_fusion.31), calls=%async_computation | async-start | bytes 3145728 | tf_op jit(solution)/shard_map/all_to_all | solution.py:441
  92.0 55.6 %collective-permute-start = (bf16[8,192,256]{2,1,0:T(8,128)(2,1)}, bf16[8,192,256]{2,1,0:T(8,128)(2,1)}, u32[]{:S(2)}, u32[]{:S(2)}) collective-permute-start(bf16[8,192,256]{2,1,0:T(8,128)(2,1)} %get-tuple-element.199), channel_id=1, source_target_pairs={{0,1},{1,0},{2,3},{3,2},{4,5},{5,4},{6,7},{7,6},{8,9},{9,8},{10,11... | collective-permute-start | bytes 2359304 | tf_op jit(solution)/shard_map/ppermute | solution.py:433
  93.8 107.0 %collective-permute-start.14 = (bf16[8,192,256]{2,1,0:T(8,128)(2,1)}, bf16[8,192,256]{2,1,0:T(8,128)(2,1)}, u32[]{:S(2)}, u32[]{:S(2)}) collective-permute-start(bf16[8,192,256]{2,1,0:T(8,128)(2,1)} %get-tuple-element.181), channel_id=1, source_target_pairs={{0,3},{1,2},{2,1},{3,0},{4,7},{5,6},{6,5},{7,4},{8,11},{9,10},{10,... | collective-permute-start | bytes 2359304 | tf_op jit(solution)/shard_map/ppermute | solution.py:433
  95.3 105.5 %collective-permute-start.13 = (bf16[8,192,256]{2,1,0:T(8,128)(2,1)}, bf16[8,192,256]{2,1,0:T(8,128)(2,1)}, u32[]{:S(2)}, u32[]{:S(2)}) collective-permute-start(bf16[8,192,256]{2,1,0:T(8,128)(2,1)} %get-tuple-element.182), channel_id=1, source_target_pairs={{0,2},{1,3},{2,0},{3,1},{4,6},{5,7},{6,4},{7,5},{8,10},{9,11},{10,... | collective-permute-start | bytes 2359304 | tf_op jit(solution)/shard_map/ppermute | solution.py:433
  120.1 80.8 %collective-permute-start.12 = (bf16[8,192,256]{2,1,0:T(8,128)(2,1)}, bf16[8,192,256]{2,1,0:T(8,128)(2,1)}, u32[]{:S(2)}, u32[]{:S(2)}) collective-permute-start(bf16[8,192,256]{2,1,0:T(8,128)(2,1)} %get-tuple-element.183), channel_id=1, source_target_pairs={{0,1},{1,0},{2,3},{3,2},{4,5},{5,4},{6,7},{7,6},{8,9},{9,8},{10,11... | collective-permute-start | bytes 2359304 | tf_op jit(solution)/shard_map/ppermute | solution.py:433
  141.3 52.6 %all-to-all-start.1 = ((bf16[32,64,384]{2,1,0:T(8,128)(2,1)}), bf16[32,64,384]{2,1,0:T(8,128)(2,1)S(1)}, u32[]{:S(2)}, u32[]{:S(2)}) async-start(bf16[32,64,384]{2,1,0:T(8,128)(2,1)} %copy_bitcast_fusion.29), calls=%async_computation.1 | async-start | bytes 3145728 | tf_op jit(solution)/shard_map/all_to_all | solution.py:441
  193.9 44.4 %all-to-all-start.2 = ((bf16[32,64,384]{2,1,0:T(8,128)(2,1)}), bf16[32,64,384]{2,1,0:T(8,128)(2,1)S(1)}, u32[]{:S(2)}, u32[]{:S(2)}) async-start(bf16[32,64,384]{2,1,0:T(8,128)(2,1)} %copy_bitcast_fusion.27), calls=%async_computation.2 | async-start | bytes 3145728 | tf_op jit(solution)/shard_map/all_to_all | solution.py:441
  238.3 52.9 %all-to-all-start.3 = ((bf16[32,64,384]{2,1,0:T(8,128)(2,1)}), bf16[32,64,384]{2,1,0:T(8,128)(2,1)}, u32[]{:S(2)}, u32[]{:S(2)}) async-start(bf16[32,64,384]{2,1,0:T(8,128)(2,1)} %copy_bitcast_fusion.25), calls=%async_computation.3 | async-start | bytes 3145728 | tf_op jit(solution)/shard_map/all_to_all | solution.py:441
  253.4 30.7 %collective-permute-start.17 = (bf16[8,192,256]{2,1,0:T(8,128)(2,1)}, bf16[8,192,256]{2,1,0:T(8,128)(2,1)}, u32[]{:S(2)}, u32[]{:S(2)}) collective-permute-start(bf16[8,192,256]{2,1,0:T(8,128)(2,1)} %get-tuple-element.177), channel_id=1, source_target_pairs={{0,3},{1,2},{2,1},{3,0},{4,7},{5,6},{6,5},{7,4},{8,11},{9,10},{10,... | collective-permute-start | bytes 2359304 | tf_op jit(solution)/shard_map/ppermute | solution.py:433
  256.1 42.7 %collective-permute-start.16 = (bf16[8,192,256]{2,1,0:T(8,128)(2,1)}, bf16[8,192,256]{2,1,0:T(8,128)(2,1)}, u32[]{:S(2)}, u32[]{:S(2)}) collective-permute-start(bf16[8,192,256]{2,1,0:T(8,128)(2,1)} %get-tuple-element.178), channel_id=1, source_target_pairs={{0,2},{1,3},{2,0},{3,1},{4,6},{5,7},{6,4},{7,5},{8,10},{9,11},{10,... | collective-permute-start | bytes 2359304 | tf_op jit(solution)/shard_map/ppermute | solution.py:433
  256.7 43.8 %collective-permute-start.15 = (bf16[8,192,256]{2,1,0:T(8,128)(2,1)}, bf16[8,192,256]{2,1,0:T(8,128)(2,1)}, u32[]{:S(2)}, u32[]{:S(2)}) collective-permute-start(bf16[8,192,256]{2,1,0:T(8,128)(2,1)} %get-tuple-element.179), channel_id=1, source_target_pairs={{0,1},{1,0},{2,3},{3,2},{4,5},{5,4},{6,7},{7,6},{8,9},{9,8},{10,11... | collective-permute-start | bytes 2359304 | tf_op jit(solution)/shard_map/ppermute | solution.py:433
  258.6 59.2 %collective-permute-start.20 = (bf16[8,192,256]{2,1,0:T(8,128)(2,1)}, bf16[8,192,256]{2,1,0:T(8,128)(2,1)}, u32[]{:S(2)}, u32[]{:S(2)}) collective-permute-start(bf16[8,192,256]{2,1,0:T(8,128)(2,1)} %get-tuple-element.173), channel_id=1, source_target_pairs={{0,3},{1,2},{2,1},{3,0},{4,7},{5,6},{6,5},{7,4},{8,11},{9,10},{10,... | collective-permute-start | bytes 2359304 | tf_op jit(solution)/shard_map/ppermute | solution.py:433
  261.4 71.1 %collective-permute-start.19 = (bf16[8,192,256]{2,1,0:T(8,128)(2,1)}, bf16[8,192,256]{2,1,0:T(8,128)(2,1)}, u32[]{:S(2)}, u32[]{:S(2)}) collective-permute-start(bf16[8,192,256]{2,1,0:T(8,128)(2,1)} %get-tuple-element.174), channel_id=1, source_target_pairs={{0,2},{1,3},{2,0},{3,1},{4,6},{5,7},{6,4},{7,5},{8,10},{9,11},{10,... | collective-permute-start | bytes 2359304 | tf_op jit(solution)/shard_map/ppermute | solution.py:433
  284.0 49.7 %collective-permute-start.18 = (bf16[8,192,256]{2,1,0:T(8,128)(2,1)}, bf16[8,192,256]{2,1,0:T(8,128)(2,1)}, u32[]{:S(2)}, u32[]{:S(2)}) collective-permute-start(bf16[8,192,256]{2,1,0:T(8,128)(2,1)} %get-tuple-element.175), channel_id=1, source_target_pairs={{0,1},{1,0},{2,3},{3,2},{4,5},{5,4},{6,7},{7,6},{8,9},{9,8},{10,11... | collective-permute-start | bytes 2359304 | tf_op jit(solution)/shard_map/ppermute | solution.py:433
  368.9 41.8 %all-to-all-start.5 = ((bf16[32,64,384]{2,1,0:T(8,128)(2,1)}), bf16[32,64,384]{2,1,0:T(8,128)(2,1)S(1)}, u32[]{:S(2)}, u32[]{:S(2)}) async-start(bf16[32,64,384]{2,1,0:T(8,128)(2,1)} %bitcast.328), calls=%async_computation.5 | async-start | bytes 3145728 | tf_op jit(solution)/shard_map/all_to_all | solution.py:441
  411.9 41.6 %all-to-all-start.7 = ((bf16[32,64,384]{2,1,0:T(8,128)(2,1)}), bf16[32,64,384]{2,1,0:T(8,128)(2,1)S(1)}, u32[]{:S(2)}, u32[]{:S(2)}) async-start(bf16[32,64,384]{2,1,0:T(8,128)(2,1)} %bitcast.342), calls=%async_computation.7 | async-start | bytes 3145728 | tf_op jit(solution)/shard_map/all_to_all | solution.py:441
  453.5 42.2 %all-to-all-start.6 = ((bf16[32,64,384]{2,1,0:T(8,128)(2,1)}), bf16[32,64,384]{2,1,0:T(8,128)(2,1)S(1)}, u32[]{:S(2)}, u32[]{:S(2)}) async-start(bf16[32,64,384]{2,1,0:T(8,128)(2,1)} %bitcast.340), calls=%async_computation.6 | async-start | bytes 3145728 | tf_op jit(solution)/shard_map/all_to_all | solution.py:441
  468.6 148.0 %collective-permute-start.5 = (bf16[8,192,256]{2,1,0:T(8,128)(2,1)}, bf16[8,192,256]{2,1,0:T(8,128)(2,1)}, u32[]{:S(2)}, u32[]{:S(2)}) collective-permute-start(bf16[8,192,256]{2,1,0:T(8,128)(2,1)} %get-tuple-element.193), channel_id=1, source_target_pairs={{0,3},{1,2},{2,1},{3,0},{4,7},{5,6},{6,5},{7,4},{8,11},{9,10},{10,... | collective-permute-start | bytes 2359304 | tf_op jit(solution)/shard_map/ppermute | solution.py:433
  471.4 152.9 %collective-permute-start.4 = (bf16[8,192,256]{2,1,0:T(8,128)(2,1)}, bf16[8,192,256]{2,1,0:T(8,128)(2,1)}, u32[]{:S(2)}, u32[]{:S(2)}) collective-permute-start(bf16[8,192,256]{2,1,0:T(8,128)(2,1)} %get-tuple-element.194), channel_id=1, source_target_pairs={{0,2},{1,3},{2,0},{3,1},{4,6},{5,7},{6,4},{7,5},{8,10},{9,11},{10,... | collective-permute-start | bytes 2359304 | tf_op jit(solution)/shard_map/ppermute | solution.py:433
  471.9 152.3 %collective-permute-start.3 = (bf16[8,192,256]{2,1,0:T(8,128)(2,1)}, bf16[8,192,256]{2,1,0:T(8,128)(2,1)}, u32[]{:S(2)}, u32[]{:S(2)}) collective-permute-start(bf16[8,192,256]{2,1,0:T(8,128)(2,1)} %get-tuple-element.195), channel_id=1, source_target_pairs={{0,1},{1,0},{2,3},{3,2},{4,5},{5,4},{6,7},{7,6},{8,9},{9,8},{10,11... | collective-permute-start | bytes 2359304 | tf_op jit(solution)/shard_map/ppermute | solution.py:433
  473.9 203.5 %collective-permute-start.26 = (bf16[8,192,256]{2,1,0:T(8,128)(2,1)}, bf16[8,192,256]{2,1,0:T(8,128)(2,1)}, u32[]{:S(2)}, u32[]{:S(2)}) collective-permute-start(bf16[8,192,256]{2,1,0:T(8,128)(2,1)} %get-tuple-element.169), channel_id=1, source_target_pairs={{0,3},{1,2},{2,1},{3,0},{4,7},{5,6},{6,5},{7,4},{8,11},{9,10},{10,... | collective-permute-start | bytes 2359304 | tf_op jit(solution)/shard_map/ppermute | solution.py:433
  476.7 200.8 %collective-permute-start.25 = (bf16[8,192,256]{2,1,0:T(8,128)(2,1)}, bf16[8,192,256]{2,1,0:T(8,128)(2,1)}, u32[]{:S(2)}, u32[]{:S(2)}) collective-permute-start(bf16[8,192,256]{2,1,0:T(8,128)(2,1)} %get-tuple-element.170), channel_id=1, source_target_pairs={{0,2},{1,3},{2,0},{3,1},{4,6},{5,7},{6,4},{7,5},{8,10},{9,11},{10,... | collective-permute-start | bytes 2359304 | tf_op jit(solution)/shard_map/ppermute | solution.py:433
  495.7 68.9 %all-to-all-start.4 = ((bf16[32,64,384]{2,1,0:T(8,128)(2,1)}), bf16[32,64,384]{2,1,0:T(8,128)(2,1)S(1)}, u32[]{:S(2)}, u32[]{:S(2)}) async-start(bf16[32,64,384]{2,1,0:T(8,128)(2,1)} %bitcast.341), calls=%async_computation.4 | async-start | bytes 3145728 | tf_op jit(solution)/shard_map/all_to_all | solution.py:441
  565.7 52.8 %all-to-all-start.9 = ((bf16[32,64,384]{2,1,0:T(8,128)(2,1)}), bf16[32,64,384]{2,1,0:T(8,128)(2,1)S(1)}, u32[]{:S(2)}, u32[]{:S(2)}) async-start(bf16[32,64,384]{2,1,0:T(8,128)(2,1)} %copy_bitcast_fusion.13), calls=%async_computation.9 | async-start | bytes 3145728 | tf_op jit(solution)/shard_map/all_to_all | solution.py:441
  616.6 60.9 %collective-permute-start.24 = (bf16[8,192,256]{2,1,0:T(8,128)(2,1)}, bf16[8,192,256]{2,1,0:T(8,128)(2,1)}, u32[]{:S(2)}, u32[]{:S(2)}) collective-permute-start(bf16[8,192,256]{2,1,0:T(8,128)(2,1)} %get-tuple-element.171), channel_id=1, source_target_pairs={{0,1},{1,0},{2,3},{3,2},{4,5},{5,4},{6,7},{7,6},{8,9},{9,8},{10,11... | collective-permute-start | bytes 2359304 | tf_op jit(solution)/shard_map/ppermute | solution.py:433
  619.6 51.8 %all-to-all-start.8 = ((bf16[32,64,384]{2,1,0:T(8,128)(2,1)}), bf16[32,64,384]{2,1,0:T(8,128)(2,1)S(1)}, u32[]{:S(2)}, u32[]{:S(2)}) async-start(bf16[32,64,384]{2,1,0:T(8,128)(2,1)} %copy_bitcast_fusion.15), calls=%async_computation.8 | async-start | bytes 3145728 | tf_op jit(solution)/shard_map/all_to_all | solution.py:441
  671.4 51.7 %all-to-all-start.10 = ((bf16[32,64,384]{2,1,0:T(8,128)(2,1)}), bf16[32,64,384]{2,1,0:T(8,128)(2,1)S(1)}, u32[]{:S(2)}, u32[]{:S(2)}) async-start(bf16[32,64,384]{2,1,0:T(8,128)(2,1)} %copy_bitcast_fusion.11), calls=%async_computation.10 | async-start | bytes 3145728 | tf_op jit(solution)/shard_map/all_to_all | solution.py:441
  723.1 106.7 %all-to-all-start.11 = ((bf16[32,64,384]{2,1,0:T(8,128)(2,1)}), bf16[32,64,384]{2,1,0:T(8,128)(2,1)}, u32[]{:S(2)}, u32[]{:S(2)}) async-start(bf16[32,64,384]{2,1,0:T(8,128)(2,1)} %copy_bitcast_fusion.9), calls=%async_computation.11 | async-start | bytes 3145728 | tf_op jit(solution)/shard_map/all_to_all | solution.py:441
  729.2 36.6 %collective-permute-start.33 = (bf16[8,192,256]{2,1,0:T(8,128)(2,1)}, bf16[8,192,256]{2,1,0:T(8,128)(2,1)}, u32[]{:S(2)}, u32[]{:S(2)}) collective-permute-start(bf16[8,192,256]{2,1,0:T(8,128)(2,1)} %get-tuple-element.105), channel_id=1, source_target_pairs={{1,0},{0,1},{3,2},{2,3},{5,4},{4,5},{7,6},{6,7},{9,8},{8,9},{11,10... | collective-permute-start | bytes 2359304 | tf_op jit(solution)/shard_map/ppermute | solution.py:438
  734.1 38.2 %collective-permute-start.34 = (bf16[8,192,256]{2,1,0:T(8,128)(2,1)}, bf16[8,192,256]{2,1,0:T(8,128)(2,1)S(1)}, u32[]{:S(2)}, u32[]{:S(2)}) collective-permute-start(bf16[8,192,256]{2,1,0:T(8,128)(2,1)} %get-tuple-element.106), channel_id=1, source_target_pairs={{2,0},{3,1},{0,2},{1,3},{6,4},{7,5},{4,6},{5,7},{10,8},{11,9},{8,1... | collective-permute-start | bytes 2359304 | tf_op jit(solution)/shard_map/ppermute | solution.py:438
  735.7 48.1 %collective-permute-start.35 = (bf16[8,192,256]{2,1,0:T(8,128)(2,1)}, bf16[8,192,256]{2,1,0:T(8,128)(2,1)S(1)}, u32[]{:S(2)}, u32[]{:S(2)}) collective-permute-start(bf16[8,192,256]{2,1,0:T(8,128)(2,1)} %get-tuple-element.107), channel_id=1, source_target_pairs={{3,0},{2,1},{1,2},{0,3},{7,4},{6,5},{5,6},{4,7},{11,8},{10,9},{9,1... | collective-permute-start | bytes 2359304 | tf_op jit(solution)/shard_map/ppermute | solution.py:438
  736.0 63.9 %collective-permute-start.30 = (bf16[8,192,256]{2,1,0:T(8,128)(2,1)}, bf16[8,192,256]{2,1,0:T(8,128)(2,1)S(1)}, u32[]{:S(2)}, u32[]{:S(2)}) collective-permute-start(bf16[8,192,256]{2,1,0:T(8,128)(2,1)} %get-tuple-element.100), channel_id=1, source_target_pairs={{1,0},{0,1},{3,2},{2,3},{5,4},{4,5},{7,6},{6,7},{9,8},{8,9},{11,10... | collective-permute-start | bytes 2359304 | tf_op jit(solution)/shard_map/ppermute | solution.py:438
  737.7 64.2 %collective-permute-start.31 = (bf16[8,192,256]{2,1,0:T(8,128)(2,1)}, bf16[8,192,256]{2,1,0:T(8,128)(2,1)S(1)}, u32[]{:S(2)}, u32[]{:S(2)}) collective-permute-start(bf16[8,192,256]{2,1,0:T(8,128)(2,1)} %get-tuple-element.101), channel_id=1, source_target_pairs={{2,0},{3,1},{0,2},{1,3},{6,4},{7,5},{4,6},{5,7},{10,8},{11,9},{8,1... | collective-permute-start | bytes 2359304 | tf_op jit(solution)/shard_map/ppermute | solution.py:438
  765.7 51.9 %collective-permute-start.32 = (bf16[8,192,256]{2,1,0:T(8,128)(2,1)}, bf16[8,192,256]{2,1,0:T(8,128)(2,1)S(1)}, u32[]{:S(2)}, u32[]{:S(2)}) collective-permute-start(bf16[8,192,256]{2,1,0:T(8,128)(2,1)} %get-tuple-element.102), channel_id=1, source_target_pairs={{3,0},{2,1},{1,2},{0,3},{7,4},{6,5},{5,6},{4,7},{11,8},{10,9},{9,1... | collective-permute-start | bytes 2359304 | tf_op jit(solution)/shard_map/ppermute | solution.py:438
  772.3 61.4 %collective-permute-start.21 = (bf16[8,192,256]{2,1,0:T(8,128)(2,1)}, bf16[8,192,256]{2,1,0:T(8,128)(2,1)}, u32[]{:S(2)}, u32[]{:S(2)}) collective-permute-start(bf16[8,192,256]{2,1,0:T(8,128)(2,1)} %get-tuple-element.89), channel_id=1, source_target_pairs={{1,0},{0,1},{3,2},{2,3},{5,4},{4,5},{7,6},{6,7},{9,8},{8,9},{11,10... | collective-permute-start | bytes 2359304 | tf_op jit(solution)/shard_map/ppermute | solution.py:438
  783.8 93.8 %collective-permute-start.22 = (bf16[8,192,256]{2,1,0:T(8,128)(2,1)}, bf16[8,192,256]{2,1,0:T(8,128)(2,1)}, u32[]{:S(2)}, u32[]{:S(2)}) collective-permute-start(bf16[8,192,256]{2,1,0:T(8,128)(2,1)} %get-tuple-element.90), channel_id=1, source_target_pairs={{2,0},{3,1},{0,2},{1,3},{6,4},{7,5},{4,6},{5,7},{10,8},{11,9},{8,1... | collective-permute-start | bytes 2359304 | tf_op jit(solution)/shard_map/ppermute | solution.py:438
  799.9 77.8 %collective-permute-start.23 = (bf16[8,192,256]{2,1,0:T(8,128)(2,1)}, bf16[8,192,256]{2,1,0:T(8,128)(2,1)}, u32[]{:S(2)}, u32[]{:S(2)}) collective-permute-start(bf16[8,192,256]{2,1,0:T(8,128)(2,1)} %get-tuple-element.91), channel_id=1, source_target_pairs={{3,0},{2,1},{1,2},{0,3},{7,4},{6,5},{5,6},{4,7},{11,8},{10,9},{9,1... | collective-permute-start | bytes 2359304 | tf_op jit(solution)/shard_map/ppermute | solution.py:438
  801.9 75.8 %collective-permute-start.27 = (bf16[8,192,256]{2,1,0:T(8,128)(2,1)}, bf16[8,192,256]{2,1,0:T(8,128)(2,1)}, u32[]{:S(2)}, u32[]{:S(2)}) collective-permute-start(bf16[8,192,256]{2,1,0:T(8,128)(2,1)} %get-tuple-element.95), channel_id=1, source_target_pairs={{1,0},{0,1},{3,2},{2,3},{5,4},{4,5},{7,6},{6,7},{9,8},{8,9},{11,10... | collective-permute-start | bytes 2359304 | tf_op jit(solution)/shard_map/ppermute | solution.py:438
  817.6 60.1 %collective-permute-start.28 = (bf16[8,192,256]{2,1,0:T(8,128)(2,1)}, bf16[8,192,256]{2,1,0:T(8,128)(2,1)}, u32[]{:S(2)}, u32[]{:S(2)}) collective-permute-start(bf16[8,192,256]{2,1,0:T(8,128)(2,1)} %get-tuple-element.96), channel_id=1, source_target_pairs={{2,0},{3,1},{0,2},{1,3},{6,4},{7,5},{4,6},{5,7},{10,8},{11,9},{8,1... | collective-permute-start | bytes 2359304 | tf_op jit(solution)/shard_map/ppermute | solution.py:438
  833.7 57.0 %collective-permute-start.29 = (bf16[8,192,256]{2,1,0:T(8,128)(2,1)S(1)}, bf16[8,192,256]{2,1,0:T(8,128)(2,1)S(1)}, u32[]{:S(2)}, u32[]{:S(2)}) collective-permute-start(bf16[8,192,256]{2,1,0:T(8,128)(2,1)S(1)} %copy-done.37), channel_id=1, source_target_pairs={{3,0},{2,1},{1,2},{0,3},{7,4},{6,5},{5,6},{4,7},{11,8},{10,9},{9,1... | collective-permute-start | bytes 2359304 | tf_op jit(solution)/shard_map/ppermute | solution.py:438
  873.2 41.5 %all-to-all-start.12 = ((bf16[32,64,384]{2,1,0:T(8,128)(2,1)}), bf16[32,64,384]{2,1,0:T(8,128)(2,1)S(1)}, u32[]{:S(2)}, u32[]{:S(2)}) async-start(bf16[32,64,384]{2,1,0:T(8,128)(2,1)} %bitcast.321), calls=%async_computation.12 | async-start | bytes 3145728 | tf_op jit(solution)/shard_map/all_to_all | solution.py:441
  877.2 209.2 %all-reduce.11.cloned.1.call-start = ((), (), s32[]{:S(2)}) async-start(), calls=%async_computation.16 | async-start | bytes 3743744 | tf_op jit(solution)/shard_map/psum | solution.py:571
  914.7 50.2 %all-to-all-start.13 = ((bf16[32,64,384]{2,1,0:T(8,128)(2,1)}), bf16[32,64,384]{2,1,0:T(8,128)(2,1)S(1)}, u32[]{:S(2)}, u32[]{:S(2)}) async-start(bf16[32,64,384]{2,1,0:T(8,128)(2,1)} %bitcast.320), calls=%async_computation.13 | async-start | bytes 3145728 | tf_op jit(solution)/shard_map/all_to_all | solution.py:441
  931.7 120.5 %collective-permute-start.36 = (bf16[8,192,256]{2,1,0:T(8,128)(2,1)}, bf16[8,192,256]{2,1,0:T(8,128)(2,1)}, u32[]{:S(2)}, u32[]{:S(2)}) collective-permute-start(bf16[8,192,256]{2,1,0:T(8,128)(2,1)} %get-tuple-element.119), channel_id=1, source_target_pairs={{1,0},{0,1},{3,2},{2,3},{5,4},{4,5},{7,6},{6,7},{9,8},{8,9},{11,10... | collective-permute-start | bytes 2359304 | tf_op jit(solution)/shard_map/ppermute | solution.py:438
  933.5 161.6 %collective-permute-start.37 = (bf16[8,192,256]{2,1,0:T(8,128)(2,1)}, bf16[8,192,256]{2,1,0:T(8,128)(2,1)}, u32[]{:S(2)}, u32[]{:S(2)}) collective-permute-start(bf16[8,192,256]{2,1,0:T(8,128)(2,1)} %get-tuple-element.120), channel_id=1, source_target_pairs={{2,0},{3,1},{0,2},{1,3},{6,4},{7,5},{4,6},{5,7},{10,8},{11,9},{8,1... | collective-permute-start | bytes 2359304 | tf_op jit(solution)/shard_map/ppermute | solution.py:438
  934.9 161.2 %collective-permute-start.38 = (bf16[8,192,256]{2,1,0:T(8,128)(2,1)}, bf16[8,192,256]{2,1,0:T(8,128)(2,1)}, u32[]{:S(2)}, u32[]{:S(2)}) collective-permute-start(bf16[8,192,256]{2,1,0:T(8,128)(2,1)} %get-tuple-element.121), channel_id=1, source_target_pairs={{3,0},{2,1},{1,2},{0,3},{7,4},{6,5},{5,6},{4,7},{11,8},{10,9},{9,1... | collective-permute-start | bytes 2359304 | tf_op jit(solution)/shard_map/ppermute | solution.py:438
  964.9 42.4 %all-to-all-start.14 = ((bf16[32,64,384]{2,1,0:T(8,128)(2,1)}), bf16[32,64,384]{2,1,0:T(8,128)(2,1)S(1)}, u32[]{:S(2)}, u32[]{:S(2)}) async-start(bf16[32,64,384]{2,1,0:T(8,128)(2,1)} %bitcast.319), calls=%async_computation.14 | async-start | bytes 3145728 | tf_op jit(solution)/shard_map/all_to_all | solution.py:441
  981.0 115.9 %collective-permute-start.39 = (bf16[8,192,256]{2,1,0:T(8,128)(2,1)}, bf16[8,192,256]{2,1,0:T(8,128)(2,1)}, u32[]{:S(2)}, u32[]{:S(2)}) collective-permute-start(bf16[8,192,256]{2,1,0:T(8,128)(2,1)} %get-tuple-element.125), channel_id=1, source_target_pairs={{1,0},{0,1},{3,2},{2,3},{5,4},{4,5},{7,6},{6,7},{9,8},{8,9},{11,10... | collective-permute-start | bytes 2359304 | tf_op jit(solution)/shard_map/ppermute | solution.py:438
  982.8 115.8 %collective-permute-start.40 = (bf16[8,192,256]{2,1,0:T(8,128)(2,1)}, bf16[8,192,256]{2,1,0:T(8,128)(2,1)}, u32[]{:S(2)}, u32[]{:S(2)}) collective-permute-start(bf16[8,192,256]{2,1,0:T(8,128)(2,1)} %get-tuple-element.126), channel_id=1, source_target_pairs={{2,0},{3,1},{0,2},{1,3},{6,4},{7,5},{4,6},{5,7},{10,8},{11,9},{8,1... | collective-permute-start | bytes 2359304 | tf_op jit(solution)/shard_map/ppermute | solution.py:438
  1007.4 43.5 %all-to-all-start.15 = ((bf16[32,64,384]{2,1,0:T(8,128)(2,1)}), bf16[32,64,384]{2,1,0:T(8,128)(2,1)S(1)}, u32[]{:S(2)}, u32[]{:S(2)}) async-start(bf16[32,64,384]{2,1,0:T(8,128)(2,1)} %bitcast.318), calls=%async_computation.15 | async-start | bytes 3145728 | tf_op jit(solution)/shard_map/all_to_all | solution.py:441
  1052.2 47.5 %collective-permute-start.41 = (bf16[8,192,256]{2,1,0:T(8,128)(2,1)}, bf16[8,192,256]{2,1,0:T(8,128)(2,1)}, u32[]{:S(2)}, u32[]{:S(2)}) collective-permute-start(bf16[8,192,256]{2,1,0:T(8,128)(2,1)} %get-tuple-element.127), channel_id=1, source_target_pairs={{3,0},{2,1},{1,2},{0,3},{7,4},{6,5},{5,6},{4,7},{11,8},{10,9},{9,1... | collective-permute-start | bytes 2359304 | tf_op jit(solution)/shard_map/ppermute | solution.py:438
  1096.2 37.3 %collective-permute-start.43 = (bf16[8,192,256]{2,1,0:T(8,128)(2,1)S(1)}, bf16[8,192,256]{2,1,0:T(8,128)(2,1)S(1)}, u32[]{:S(2)}, u32[]{:S(2)}) collective-permute-start(bf16[8,192,256]{2,1,0:T(8,128)(2,1)S(1)} %copy-done.41), channel_id=1, source_target_pairs={{2,0},{3,1},{0,2},{1,3},{6,4},{7,5},{4,6},{5,7},{10,8},{11,9},{8,1... | collective-permute-start | bytes 2359304 | tf_op jit(solution)/shard_map/ppermute | solution.py:438
  1096.8 38.0 %collective-permute-start.44 = (bf16[8,192,256]{2,1,0:T(8,128)(2,1)S(1)}, bf16[8,192,256]{2,1,0:T(8,128)(2,1)S(1)}, u32[]{:S(2)}, u32[]{:S(2)}) collective-permute-start(bf16[8,192,256]{2,1,0:T(8,128)(2,1)S(1)} %copy-done.39), channel_id=1, source_target_pairs={{3,0},{2,1},{1,2},{0,3},{7,4},{6,5},{5,6},{4,7},{11,8},{10,9},{9,1... | collective-permute-start | bytes 2359304 | tf_op jit(solution)/shard_map/ppermute | solution.py:438
  1098.6 50.9 %collective-permute-start.45 = (bf16[8,192,256]{2,1,0:T(8,128)(2,1)}, bf16[8,192,256]{2,1,0:T(8,128)(2,1)S(1)}, u32[]{:S(2)}, u32[]{:S(2)}) collective-permute-start(bf16[8,192,256]{2,1,0:T(8,128)(2,1)} %get-tuple-element.137), channel_id=1, source_target_pairs={{1,0},{0,1},{3,2},{2,3},{5,4},{4,5},{7,6},{6,7},{9,8},{8,9},{11,10... | collective-permute-start | bytes 2359304 | tf_op jit(solution)/shard_map/ppermute | solution.py:438
  1099.7 65.7 %collective-permute-start.46 = (bf16[8,192,256]{2,1,0:T(8,128)(2,1)}, bf16[8,192,256]{2,1,0:T(8,128)(2,1)S(1)}, u32[]{:S(2)}, u32[]{:S(2)}) collective-permute-start(bf16[8,192,256]{2,1,0:T(8,128)(2,1)} %get-tuple-element.138), channel_id=1, source_target_pairs={{2,0},{3,1},{0,2},{1,3},{6,4},{7,5},{4,6},{5,7},{10,8},{11,9},{8,1... | collective-permute-start | bytes 2359304 | tf_op jit(solution)/shard_map/ppermute | solution.py:438
  1115.7 51.0 %collective-permute-start.47 = (bf16[8,192,256]{2,1,0:T(8,128)(2,1)S(1)}, bf16[8,192,256]{2,1,0:T(8,128)(2,1)S(1)}, u32[]{:S(2)}, u32[]{:S(2)}) collective-permute-start(bf16[8,192,256]{2,1,0:T(8,128)(2,1)S(1)} %copy-done.40), channel_id=1, source_target_pairs={{3,0},{2,1},{1,2},{0,3},{7,4},{6,5},{5,6},{4,7},{11,8},{10,9},{9,1... | collective-permute-start | bytes 2359304 | tf_op jit(solution)/shard_map/ppermute | solution.py:438
  (48 other events, 385.4 us)
Sparse Core Ops, SparseCore 0:
  910.3 176.0 all-reduce.10

commit v2 on v1

--- a/solution.py
+++ b/solution.py
@@ -20,6 +20,9 @@
 EVERY = ("row", "col")
 VMEM_BYTES = 56 * 2**20
 CHUNK_ROWS = 8
+COT_EARLY = 0
+OUT_LAG = 2
+OUT_LATE = 2
 FIRST_US = 60
 TOKEN_US = 100
 LAST_US = 60
@@ -462,7 +465,10 @@
 
     def field_pieces(field, at):
         split = split_rows(field, target, own_rows, at * chunk, chunk, pair)
-        return [[send(rows[slot], slot) for slot in range(col_count)] for rows in split]
+        return [[rows[slot] for slot in range(col_count)] for rows in split]
+
+    def send_all(pieces):
+        return [send(piece, slot) for slot, piece in enumerate(pieces)]
 
     def to_modes(spectrum):
         parted = spectrum.reshape(chunk, devices, own_modes, doubled).transpose(1, 0, 2, 3)
@@ -490,8 +496,10 @@
     spectrum_shape = shape(chunk, KW, doubled)
     rows_shape = shape(own_modes, devices * chunk, doubled)
 
-    weather_now = sum([field_pieces(weather, at) for at in range(0, chunks, pair)], [])
-    cot_now = sum([field_pieces(cotangent, at) for at in range(0, chunks, pair)], [])
+    starts = range(0, chunks, pair)
+    weather_now = [send_all(x) for at in starts for x in field_pieces(weather, at)]
+    cot_parts = [x for at in starts for x in field_pieces(cotangent, at)]
+    cot_now = [send_all(x) for x in cot_parts]
     spectra = []
     for at in range(chunks):
         (spectrum,) = call_rows(
@@ -503,6 +511,7 @@
             [forward_plain],
             [spectrum_shape],
             [],
+            waited=[cot_parts[0][0], cot_parts[-1][0]] if at == chunks - 1 else [],
         )
         spectra.append(to_modes(spectrum))
 
@@ -516,7 +525,7 @@
         [rows_shape] * chunks
         + [shape(*mode_dims), shape(*mode_dims), shape(*mode_dims, kind=F32), shape(*mode_dims, kind=F32)],
         [],
-        waited=[piece for pieces in cot_now[: chunks // 2] for piece in pieces],
+        waited=[piece for pieces in cot_now[:COT_EARLY] for piece in pieces],
     )
     back, saved = results[:chunks], results[chunks:]
 
@@ -539,6 +548,7 @@
             [piece_shape] * col_count
             + [shape(chunk, col_count, channels, local_cols, kind=F32), spectrum_shape],
             [shape(hidden_units, channels, kind=F32)] * 2,
+            waited=outputs[at - OUT_LAG] if at >= OUT_LAG else [],
         )
         spectrum = results[col_count + 1]
         outputs.append([send_back(results[slot], slot) for slot in range(col_count)])
@@ -546,7 +556,7 @@
         grad_spectra.append(to_modes(spectrum))
         grad_onto = grad_onto + results[col_count + 2]
         grad_into = grad_into + results[col_count + 3]
-    early = chunks // 2
+    early = max(chunks - OUT_LATE, 0)
     results = call_modes(
         functools.partial(modes_back_kernel, chunks),
             MODES_US,
@@ -583,10 +593,12 @@
             [inverse_plain],
             [piece_shape] * col_count,
             [],
-            waited=outputs[early + at // 2] if at % 2 == 0 and early + at // 2 < chunks else [],
+            waited=outputs[early + at] if early + at < chunks else [],
         )
         grads.append([send_back(results[slot], slot) for slot in range(col_count)])
-    token_grads, packed = scale([token_grads, packed], 1.0 / height, [results[0]])
+    token_grads, packed = scale(
+        [token_grads, packed], 1.0 / height, grads[max(chunks - 2, 0)]
+    )
 
     layer_out = None
     for at in range(0, chunks, pair):

time: 1180 us -> 1130 us (0.958)
  waiting for transfers between devices: 499 us -> 432 us
    ppermute x24, waiting for transfers between devices: 130 us -> 49.1 us  [send_back(): lax.ppermute(piece, 'col', [(partner(at, slot), at) for at in range(col_c...]
    all_to_all x16, waiting for transfers between devices: 259 us -> 316 us  [exchange(): lax.all_to_all(spectrum, EVERY, split_axis=0, concat_axis=0, tiled=True)]
    ppermute x24, waiting for transfers between devices: 89.5 us -> 46.2 us  [send(): lax.ppermute(piece, 'col', [(at, partner(at, slot)) for at in range(col_c...]
  transfers between devices with their start and end apart: 65 -> 65, of which waited for: 31 -> 22; matrix products, arithmetic and copies ran while one was open for 10% -> 10% of each run, Pallas kernels for 28% -> 30%
where the time goes in v2:
time: 1130 us; the launch traced here: 1120 us
  waiting for transfers between devices  432 us (38%)
  Pallas kernels  371 us (33%)
  starting transfers between devices  159 us (14%)
  local copies, waits for them, and re-layouts  130 us (12%)
  between operations  17.5 us (2%)
    all_to_all x16, waiting for transfers between devices, exchange(): lax.all_to_all(spectrum, EVERY, split_axis=0, concat_axis=0, tiled=True)  316 us
    pallas_call x12, Pallas kernels, call_rows(): pl.pallas_call(leave_out(kernel, 1 + len(stepped) + len(fixed), len(waite...  255 us
    all_to_all x16, starting transfers between devices, exchange(): lax.all_to_all(spectrum, EVERY, split_axis=0, concat_axis=0, tiled=True)  91.9 us
    pallas_call x2, Pallas kernels, call_modes(): pl.pallas_call(leave_out(kernel, len(stepped) + len(fixed), len(waited)),...  64.8 us
    ppermute x24, waiting for transfers between devices, send_back(): lax.ppermute(piece, 'col', [(partner(at, slot), at) for at in range(col_c...  49.1 us
    ppermute x24, waiting for transfers between devices, send(): lax.ppermute(piece, 'col', [(at, partner(at, slot)) for at in range(col_c...  46.2 us
    ppermute x24, starting transfers between devices, send_back(): lax.ppermute(piece, 'col', [(partner(at, slot), at) for at in range(col_c...  35.5 us
    ppermute x24, starting transfers between devices, send(): lax.ppermute(piece, 'col', [(at, partner(at, slot)) for at in range(col_c...  31.1 us
  transfers between devices with their start and end apart: 65, of which 22 were waited for; matrix products, arithmetic and copies ran while one was open for 10% of the time, Pallas kernels for 30%

profile of v2, /device:TPU:0, one launch (start us, length us, event | category | flops | bytes accessed | tf_op | source)
XLA Modules:
  0.0 1116.4 jit_solution(1027745325508167403)
XLA Ops:
  7.7 6.8 shard_map.182
  14.5 3.2 slice_bitcast_fusion.21
  17.7 3.9 collective-permute-start.8
  27.0 6.8 shard_map.180
  33.8 6.8 shard_map.186
  40.6 7.1 shard_map.181
  61.9 9.2 shard_map.183
  73.9 18.1 %all-to-all-start = ((bf16[32,64,384]{2,1,0:T(8,128)(2,1)}), bf16[32,64,384]{2,1,0:T(8,128)(2,1)S(1)}, u32[]{:S(2)}, u32[]{:S(2)}) async-start(bf16[32,64,384]{2,1,0:T(8,128)(2,1)} %copy_bitcast_fusion.31), calls=%async_computation | async-start | bytes 3145728 | tf_op jit(solution)/shard_map/all_to_all | solution.py:444
  95.6 9.2 shard_map.184
  107.7 12.3 %collective-permute-done.2.refs_4_ = bf16[8,192,256]{2,1,0:T(8,128)(2,1)} collective-permute-done((bf16[8,192,256]{2,1,0:T(8,128)(2,1)}, bf16[8,192,256]{2,1,0:T(8,128)(2,1)}, u32[]{:S(2)}, u32[]{:S(2)}) %collective-permute-start.2) | collective-permute-done | bytes 786464 | tf_op jit(solution)/shard_map/ppermute | solution.py:436
  121.3 18.8 %all-to-all-done = bf16[32,64,384]{2,1,0:T(8,128)(2,1)S(1)} async-done(((bf16[32,64,384]{2,1,0:T(8,128)(2,1)}), bf16[32,64,384]{2,1,0:T(8,128)(2,1)S(1)}, u32[]{:S(2)}, u32[]{:S(2)}) %all-to-all-start) | async-done | bytes 1572896 | tf_op jit(solution)/shard_map/all_to_all | solution.py:444
  140.1 6.3 all-to-all-start.1
  146.4 9.2 shard_map.185
  158.5 35.4 %all-to-all-done.1 = bf16[32,64,384]{2,1,0:T(8,128)(2,1)S(1)} async-done(((bf16[32,64,384]{2,1,0:T(8,128)(2,1)}), bf16[32,64,384]{2,1,0:T(8,128)(2,1)S(1)}, u32[]{:S(2)}, u32[]{:S(2)}) %all-to-all-start.1) | async-done | bytes 1572896 | tf_op jit(solution)/shard_map/all_to_all | solution.py:444
  193.9 7.3 all-to-all-start.2
  201.2 9.2 shard_map.187
  213.3 25.3 %all-to-all-done.2 = bf16[32,64,384]{2,1,0:T(8,128)(2,1)} async-done(((bf16[32,64,384]{2,1,0:T(8,128)(2,1)}), bf16[32,64,384]{2,1,0:T(8,128)(2,1)}, u32[]{:S(2)}, u32[]{:S(2)}) %all-to-all-start.2) | async-done | bytes 1572896 | tf_op jit(solution)/shard_map/all_to_all | solution.py:444
  238.6 4.5 all-to-all-start.3
  250.9 29.8 %all-to-all-done.3 = bf16[32,64,384]{2,1,0:T(8,128)(2,1)} async-done(((bf16[32,64,384]{2,1,0:T(8,128)(2,1)}), bf16[32,64,384]{2,1,0:T(8,128)(2,1)}, u32[]{:S(2)}, u32[]{:S(2)}) %all-to-all-start.3) | async-done | bytes 1572896 | tf_op jit(solution)/shard_map/all_to_all | solution.py:444
  283.4 31.4 %shard_map.188 = (bf16[8,256,384]{2,1,0:T(8,128)(2,1)}, bf16[8,256,384]{2,1,0:T(8,128)(2,1)}, bf16[8,256,384]{2,1,0:T(8,128)(2,1)}, bf16[8,256,384]{2,1,0:T(8,12...) custom-call(bf16[8,256,384]{2,1,0:T(8,128)(2,1)} %bitcast.353, ...), custom_call_target="tpu_custom_call" | custom-call | flops 69000003584 | bytes 216000000 | tf_op jit(solution)/shard_map/pallas_call | solution.py:270
  314.8 4.0 copy.133
  318.8 4.1 all-to-all-start.5
  325.6 34.8 %all-to-all-done.5 = bf16[32,64,384]{2,1,0:T(8,128)(2,1)S(1)} async-done(((bf16[32,64,384]{2,1,0:T(8,128)(2,1)}), bf16[32,64,384]{2,1,0:T(8,128)(2,1)S(1)}, u32[]{:S(2)}, u32[]{:S(2)}) %all-to-all-start.5) | async-done | bytes 1572896 | tf_op jit(solution)/shard_map/all_to_all | solution.py:444
  360.4 4.1 all-to-all-start.7
  364.5 4.0 copy.134
  368.5 33.5 %all-to-all-done.7 = bf16[32,64,384]{2,1,0:T(8,128)(2,1)S(1)} async-done(((bf16[32,64,384]{2,1,0:T(8,128)(2,1)}), bf16[32,64,384]{2,1,0:T(8,128)(2,1)S(1)}, u32[]{:S(2)}, u32[]{:S(2)}) %all-to-all-start.7) | async-done | bytes 1572896 | tf_op jit(solution)/shard_map/all_to_all | solution.py:444
  403.2 4.6 all-to-all-start.4
  407.8 3.7 slice_bitcast_fusion.1
  421.1 3.7 slice_bitcast_fusion.25
  428.8 19.0 %collective-permute-done.29.refs_8_ = bf16[8,192,256]{2,1,0:T(8,128)(2,1)} collective-permute-done((bf16[8,192,256]{2,1,0:T(8,128)(2,1)}, bf16[8,192,256]{2,1,0:T(8,128)(2,1)}, u32[]{:S(2)}, u32[]{:S(2)}) %collective-permute-start.29) | collective-permute-done | bytes 786464 | tf_op jit(solution)/shard_map/ppermute | solution.py:436
  448.3 14.2 %collective-permute-done.28.refs_7_ = bf16[8,192,256]{2,1,0:T(8,128)(2,1)} collective-permute-done((bf16[8,192,256]{2,1,0:T(8,128)(2,1)}, bf16[8,192,256]{2,1,0:T(8,128)(2,1)}, u32[]{:S(2)}, u32[]{:S(2)}) %collective-permute-start.28) | collective-permute-done | bytes 786464 | tf_op jit(solution)/shard_map/ppermute | solution.py:436
  466.6 5.4 all-to-all-start.6
  472.0 42.9 %shard_map.191 = (bf16[8,192,256]{2,1,0:T(8,128)(2,1)}, bf16[8,192,256]{2,1,0:T(8,128)(2,1)}, bf16[8,192,256]{2,1,0:T(8,128)(2,1)}, bf16[8,192,256]{2,1,0:T(8,12...) custom-call(s32[4]{0:T(128)} %iota_xor_fusion.order.refs_0_, ...), custom_call_target="tpu_custom_call" | custom-call | flops 115000000512 | bytes 360000000 | tf_op jit(solution)/shard_map/pallas_call | solution.py:252
  522.8 25.5 %all-to-all-done.6 = bf16[32,64,384]{2,1,0:T(8,128)(2,1)} async-done(((bf16[32,64,384]{2,1,0:T(8,128)(2,1)}), bf16[32,64,384]{2,1,0:T(8,128)(2,1)}, u32[]{:S(2)}, u32[]{:S(2)}) %all-to-all-start.6) | async-done | bytes 1572896 | tf_op jit(solution)/shard_map/all_to_all | solution.py:444
  548.3 5.8 all-to-all-start.9
  554.1 42.9 %shard_map.189 = (bf16[8,192,256]{2,1,0:T(8,128)(2,1)}, bf16[8,192,256]{2,1,0:T(8,128)(2,1)}, bf16[8,192,256]{2,1,0:T(8,128)(2,1)}, bf16[8,192,256]{2,1,0:T(8,12...) custom-call(s32[4]{0:T(128)} %iota_xor_fusion.order.refs_0_, ...), custom_call_target="tpu_custom_call" | custom-call | flops 115000000512 | bytes 360000000 | tf_op jit(solution)/shard_map/pallas_call | solution.py:252
  611.0 23.4 %collective-permute-done.31.refs_18_.refs_6_ = bf16[8,192,256]{2,1,0:T(8,128)(2,1)S(1)} collective-permute-done((bf16[8,192,256]{2,1,0:T(8,128)(2,1)S(1)}, bf16[8,192,256]{2,1,0:T(8,128)(2,1)S(1)}, u32[]{:S(2)}, u32[]{:S(2)}) %collective-permute-start.31) | collective-permute-done | bytes 786464 | tf_op jit(solution)/shard_map/ppermute | solution.py:441
  639.8 4.6 all-to-all-start.8
  644.4 43.2 %shard_map.192 = (bf16[8,192,256]{2,1,0:T(8,128)(2,1)}, bf16[8,192,256]{2,1,0:T(8,128)(2,1)}, bf16[8,192,256]{2,1,0:T(8,128)(2,1)}, bf16[8,192,256]{2,1,0:T(8,12...) custom-call(s32[4]{0:T(128)} %iota_xor_fusion.order.refs_0_, ...), custom_call_target="tpu_custom_call" | custom-call | flops 115000000512 | bytes 360000000 | tf_op jit(solution)/shard_map/pallas_call | solution.py:252
  690.5 10.2 all-to-all-done.8
  700.7 6.5 all-to-all-start.11
  707.2 43.1 %shard_map.190 = (bf16[8,192,256]{2,1,0:T(8,128)(2,1)}, bf16[8,192,256]{2,1,0:T(8,128)(2,1)}, bf16[8,192,256]{2,1,0:T(8,128)(2,1)}, bf16[8,192,256]{2,1,0:T(8,12...) custom-call(s32[4]{0:T(128)} %iota_xor_fusion.order.refs_0_, ...), custom_call_target="tpu_custom_call" | custom-call | flops 115000000512 | bytes 360000000 | tf_op jit(solution)/shard_map/pallas_call | solution.py:252
  753.1 6.1 all-to-all-start.10
  773.4 7.2 shard_map.193.refs_8_
  784.7 12.0 %all-to-all-done.10 = bf16[32,64,384]{2,1,0:T(8,128)(2,1)} async-done(((bf16[32,64,384]{2,1,0:T(8,128)(2,1)}), bf16[32,64,384]{2,1,0:T(8,128)(2,1)}, u32[]{:S(2)}, u32[]{:S(2)}) %all-to-all-start.10) | async-done | bytes 1572896 | tf_op jit(solution)/shard_map/all_to_all | solution.py:444
  802.0 33.4 %shard_map.195 = (bf16[8,256,384]{2,1,0:T(8,128)(2,1)}, bf16[8,256,384]{2,1,0:T(8,128)(2,1)}, bf16[8,256,384]{2,1,0:T(8,128)(2,1)}, bf16[8,256,384]{2,1,0:T(8,12...) custom-call(bf16[8,256,384]{2,1,0:T(8,128)(2,1)} %bitcast.348, bf16[8,256,384]{2,1,0:T(8,128)(2,1)} %bitcast.347, ...), custom_call_target="tpu_custom_call" | custom-call | flops 69000003584 | bytes 216000000 | tf_op jit(solution)/shard_map/pallas_call | solution.py:270
  835.4 4.0 copy.126
  842.6 5.8 collective-permute-done.23.refs_3_.refs_11_
  849.3 7.2 shard_map.194
  867.9 11.7 %all-to-all-done.12 = bf16[32,64,384]{2,1,0:T(8,128)(2,1)S(1)} async-done(((bf16[32,64,384]{2,1,0:T(8,128)(2,1)}), bf16[32,64,384]{2,1,0:T(8,128)(2,1)S(1)}, u32[]{:S(2)}, u32[]{:S(2)}) %all-to-all-start.12) | async-done | bytes 1572896 | tf_op jit(solution)/shard_map/all_to_all | solution.py:444
  879.6 4.2 all-to-all-start.14
  885.1 11.5 %shard_map.196 = (bf16[8,192,256]{2,1,0:T(8,128)(2,1)}, bf16[8,192,256]{2,1,0:T(8,128)(2,1)}, bf16[8,192,256]{2,1,0:T(8,128)(2,1)}, bf16[8,192,256]{2,1,0:T(8,128)(2,1)}) custom-call(s32[4]{0:T(128)} %iota_xor_fusion.order.refs_0_, bf16[8,192,256]{2,1,0:T(8,128)(2,1)} %get-tuple-element.192.refs_1_, bf16[8,192,256]{2,1,0:T(8,128)(2,1)} %collective-permute-done.6.refs_2_, ...), custom_call_target="tpu_custom_call" | custom-call | flops 69000003584 | bytes 216000000 | tf_op jit(solution)/shard_map/pallas_call | solution.py:252
  899.8 28.8 %all-to-all-done.14 = bf16[32,64,384]{2,1,0:T(8,128)(2,1)S(1)} async-done(((bf16[32,64,384]{2,1,0:T(8,128)(2,1)}), bf16[32,64,384]{2,1,0:T(8,128)(2,1)S(1)}, u32[]{:S(2)}, u32[]{:S(2)}) %all-to-all-start.14) | async-done | bytes 1572896 | tf_op jit(solution)/shard_map/all_to_all | solution.py:444
  928.7 3.9 all-to-all-start.13
  933.9 11.4 %shard_map.199 = (bf16[8,192,256]{2,1,0:T(8,128)(2,1)}, bf16[8,192,256]{2,1,0:T(8,128)(2,1)}, bf16[8,192,256]{2,1,0:T(8,128)(2,1)}, bf16[8,192,256]{2,1,0:T(8,128)(2,1)}) custom-call(s32[4]{0:T(128)} %iota_xor_fusion.order.refs_0_, bf16[8,192,256]{2,1,0:T(8,128)(2,1)} %get-tuple-element.200.refs_1_, bf16[8,192,256]{2,1,0:T(8,128)(2,1)} %collective-permute-done.refs_2_, ...), custom_call_target="tpu_custom_call" | custom-call | flops 69000003584 | bytes 216000000 | tf_op jit(solution)/shard_map/pallas_call | solution.py:252
  948.8 22.9 %all-to-all-done.13 = bf16[32,64,384]{2,1,0:T(8,128)(2,1)S(1)} async-done(((bf16[32,64,384]{2,1,0:T(8,128)(2,1)}), bf16[32,64,384]{2,1,0:T(8,128)(2,1)S(1)}, u32[]{:S(2)}, u32[]{:S(2)}) %all-to-all-start.13) | async-done | bytes 1572896 | tf_op jit(solution)/shard_map/all_to_all | solution.py:444
  971.8 3.8 all-to-all-start.15
  976.9 11.4 %shard_map.197 = (bf16[8,192,256]{2,1,0:T(8,128)(2,1)}, bf16[8,192,256]{2,1,0:T(8,128)(2,1)}, bf16[8,192,256]{2,1,0:T(8,128)(2,1)}, bf16[8,192,256]{2,1,0:T(8,128)(2,1)}) custom-call(s32[4]{0:T(128)} %iota_xor_fusion.order.refs_0_, bf16[8,192,256]{2,1,0:T(8,128)(2,1)} %get-tuple-element.188.refs_1_, bf16[8,192,256]{2,1,0:T(8,128)(2,1)} %collective-permute-done.9.refs_2_, ...), custom_call_target="tpu_custom_call" | custom-call | flops 69000003584 | bytes 216000000 | tf_op jit(solution)/shard_map/pallas_call | solution.py:252
  988.3 26.8 %all-to-all-done.15 = bf16[32,64,384]{2,1,0:T(8,128)(2,1)S(1)} async-done(((bf16[32,64,384]{2,1,0:T(8,128)(2,1)}), bf16[32,64,384]{2,1,0:T(8,128)(2,1)S(1)}, u32[]{:S(2)}, u32[]{:S(2)}) %all-to-all-start.15) | async-done | bytes 1572896 | tf_op jit(solution)/shard_map/all_to_all | solution.py:444
  1022.3 11.4 %shard_map.200 = (bf16[8,192,256]{2,1,0:T(8,128)(2,1)}, bf16[8,192,256]{2,1,0:T(8,128)(2,1)}, bf16[8,192,256]{2,1,0:T(8,128)(2,1)}, bf16[8,192,256]{2,1,0:T(8,128)(2,1)}) custom-call(s32[4]{0:T(128)} %iota_xor_fusion.order.refs_0_, bf16[8,192,256]{2,1,0:T(8,128)(2,1)} %get-tuple-element.184.refs_1_, bf16[8,192,256]{2,1,0:T(8,128)(2,1)} %collective-permute-done.12.refs_2_, ...), custom_call_target="tpu_custom_call" | custom-call | flops 69000003584 | bytes 216000000 | tf_op jit(solution)/shard_map/pallas_call | solution.py:252
  1033.7 21.0 %all-reduce.11.cloned.1.call-done = (f32[1536,192]{1,0:T(8,128)}, f32[579,128]{1,0:T(8,128)}) async-done(((f32[1536,192]{1,0:T(8,128)}, f32[579,128]{1,0:T(8,128)}), (f32[1536,192]{1,0:T(8,128)}, f32[579,128]{1,0:T(8,128)})) %all-reduce.11.cloned.1.call-update) | async-done | bytes 1476112 | tf_op jit(solution)/shard_map/psum | solution.py:581
  1068.3 7.5 collective-permute-done.41.refs_7_
  1075.8 7.2 shard_map.198
  1095.7 12.4 %collective-permute-done.47 = bf16[8,192,256]{2,1,0:T(8,128)(2,1)S(1)} collective-permute-done((bf16[8,192,256]{2,1,0:T(8,128)(2,1)S(1)}, bf16[8,192,256]{2,1,0:T(8,128)(2,1)S(1)}, u32[]{:S(2)}, u32[]{:S(2)}) %collective-permute-start.47) | collective-permute-done | bytes 786464 | tf_op jit(solution)/shard_map/ppermute | solution.py:441
  (266 shorter events, 183.6 us)
Async XLA Ops:
  17.7 40.8 %collective-permute-start.8 = (bf16[8,192,256]{2,1,0:T(8,128)(2,1)S(1)}, bf16[8,192,256]{2,1,0:T(8,128)(2,1)S(1)}, u32[]{:S(2)}, u32[]{:S(2)}) collective-permute-start(bf16[8,192,256]{2,1,0:T(8,128)(2,1)S(1)} %get-tuple-element.189), channel_id=1, source_target_pairs={{0,3},{1,2},{2,1},{3,0},{4,7},{5,6},{6,5},{7,4},{8,11},{9,10},{10,... | collective-permute-start | bytes 2359304 | tf_op jit(solution)/shard_map/ppermute | solution.py:436
  21.6 36.9 %collective-permute-start.7 = (bf16[8,192,256]{2,1,0:T(8,128)(2,1)S(1)}, bf16[8,192,256]{2,1,0:T(8,128)(2,1)}, u32[]{:S(2)}, u32[]{:S(2)}) collective-permute-start(bf16[8,192,256]{2,1,0:T(8,128)(2,1)S(1)} %get-tuple-element.190), channel_id=1, source_target_pairs={{0,2},{1,3},{2,0},{3,1},{4,6},{5,7},{6,4},{7,5},{8,10},{9,11},{10,... | collective-permute-start | bytes 2359304 | tf_op jit(solution)/shard_map/ppermute | solution.py:436
  22.1 39.3 %collective-permute-start.6 = (bf16[8,192,256]{2,1,0:T(8,128)(2,1)S(1)}, bf16[8,192,256]{2,1,0:T(8,128)(2,1)}, u32[]{:S(2)}, u32[]{:S(2)}) collective-permute-start(bf16[8,192,256]{2,1,0:T(8,128)(2,1)S(1)} %get-tuple-element.191), channel_id=1, source_target_pairs={{0,1},{1,0},{2,3},{3,2},{4,5},{5,4},{6,7},{7,6},{8,9},{9,8},{10,11... | collective-permute-start | bytes 2359304 | tf_op jit(solution)/shard_map/ppermute | solution.py:436
  23.6 68.5 %collective-permute-start.11 = (bf16[8,192,256]{2,1,0:T(8,128)(2,1)}, bf16[8,192,256]{2,1,0:T(8,128)(2,1)}, u32[]{:S(2)}, u32[]{:S(2)}) collective-permute-start(bf16[8,192,256]{2,1,0:T(8,128)(2,1)} %get-tuple-element.185), channel_id=1, source_target_pairs={{0,3},{1,2},{2,1},{3,0},{4,7},{5,6},{6,5},{7,4},{8,11},{9,10},{10,... | collective-permute-start | bytes 2359304 | tf_op jit(solution)/shard_map/ppermute | solution.py:436
  26.5 67.4 %collective-permute-start.10 = (bf16[8,192,256]{2,1,0:T(8,128)(2,1)S(1)}, bf16[8,192,256]{2,1,0:T(8,128)(2,1)}, u32[]{:S(2)}, u32[]{:S(2)}) collective-permute-start(bf16[8,192,256]{2,1,0:T(8,128)(2,1)S(1)} %get-tuple-element.186), channel_id=1, source_target_pairs={{0,2},{1,3},{2,0},{3,1},{4,6},{5,7},{6,4},{7,5},{8,10},{9,11},{10,... | collective-permute-start | bytes 2359304 | tf_op jit(solution)/shard_map/ppermute | solution.py:436
  58.4 36.9 %collective-permute-start.9 = (bf16[8,192,256]{2,1,0:T(8,128)(2,1)S(1)}, bf16[8,192,256]{2,1,0:T(8,128)(2,1)}, u32[]{:S(2)}, u32[]{:S(2)}) collective-permute-start(bf16[8,192,256]{2,1,0:T(8,128)(2,1)S(1)} %get-tuple-element.187), channel_id=1, source_target_pairs={{0,1},{1,0},{2,3},{3,2},{4,5},{5,4},{6,7},{7,6},{8,9},{9,8},{10,11... | collective-permute-start | bytes 2359304 | tf_op jit(solution)/shard_map/ppermute | solution.py:436
  58.5 61.5 %collective-permute-start.2 = (bf16[8,192,256]{2,1,0:T(8,128)(2,1)}, bf16[8,192,256]{2,1,0:T(8,128)(2,1)}, u32[]{:S(2)}, u32[]{:S(2)}) collective-permute-start(bf16[8,192,256]{2,1,0:T(8,128)(2,1)} %get-tuple-element.197), channel_id=1, source_target_pairs={{0,3},{1,2},{2,1},{3,0},{4,7},{5,6},{6,5},{7,4},{8,11},{9,10},{10,... | collective-permute-start | bytes 2359304 | tf_op jit(solution)/shard_map/ppermute | solution.py:436
  61.4 85.0 %collective-permute-start.1 = (bf16[8,192,256]{2,1,0:T(8,128)(2,1)}, bf16[8,192,256]{2,1,0:T(8,128)(2,1)}, u32[]{:S(2)}, u32[]{:S(2)}) collective-permute-start(bf16[8,192,256]{2,1,0:T(8,128)(2,1)} %get-tuple-element.198), channel_id=1, source_target_pairs={{0,2},{1,3},{2,0},{3,1},{4,6},{5,7},{6,4},{7,5},{8,10},{9,11},{10,... | collective-permute-start | bytes 2359304 | tf_op jit(solution)/shard_map/ppermute | solution.py:436
  73.9 66.2 %all-to-all-start = ((bf16[32,64,384]{2,1,0:T(8,128)(2,1)}), bf16[32,64,384]{2,1,0:T(8,128)(2,1)S(1)}, u32[]{:S(2)}, u32[]{:S(2)}) async-start(bf16[32,64,384]{2,1,0:T(8,128)(2,1)} %copy_bitcast_fusion.31), calls=%async_computation | async-start | bytes 3145728 | tf_op jit(solution)/shard_map/all_to_all | solution.py:444
  92.1 54.4 %collective-permute-start = (bf16[8,192,256]{2,1,0:T(8,128)(2,1)}, bf16[8,192,256]{2,1,0:T(8,128)(2,1)}, u32[]{:S(2)}, u32[]{:S(2)}) collective-permute-start(bf16[8,192,256]{2,1,0:T(8,128)(2,1)} %get-tuple-element.199), channel_id=1, source_target_pairs={{0,1},{1,0},{2,3},{3,2},{4,5},{5,4},{6,7},{7,6},{8,9},{9,8},{10,11... | collective-permute-start | bytes 2359304 | tf_op jit(solution)/shard_map/ppermute | solution.py:436
  93.9 107.3 %collective-permute-start.14 = (bf16[8,192,256]{2,1,0:T(8,128)(2,1)}, bf16[8,192,256]{2,1,0:T(8,128)(2,1)}, u32[]{:S(2)}, u32[]{:S(2)}) collective-permute-start(bf16[8,192,256]{2,1,0:T(8,128)(2,1)} %get-tuple-element.181), channel_id=1, source_target_pairs={{0,3},{1,2},{2,1},{3,0},{4,7},{5,6},{6,5},{7,4},{8,11},{9,10},{10,... | collective-permute-start | bytes 2359304 | tf_op jit(solution)/shard_map/ppermute | solution.py:436
  95.4 105.8 %collective-permute-start.13 = (bf16[8,192,256]{2,1,0:T(8,128)(2,1)}, bf16[8,192,256]{2,1,0:T(8,128)(2,1)}, u32[]{:S(2)}, u32[]{:S(2)}) collective-permute-start(bf16[8,192,256]{2,1,0:T(8,128)(2,1)} %get-tuple-element.182), channel_id=1, source_target_pairs={{0,2},{1,3},{2,0},{3,1},{4,6},{5,7},{6,4},{7,5},{8,10},{9,11},{10,... | collective-permute-start | bytes 2359304 | tf_op jit(solution)/shard_map/ppermute | solution.py:436
  120.0 81.2 %collective-permute-start.12 = (bf16[8,192,256]{2,1,0:T(8,128)(2,1)}, bf16[8,192,256]{2,1,0:T(8,128)(2,1)}, u32[]{:S(2)}, u32[]{:S(2)}) collective-permute-start(bf16[8,192,256]{2,1,0:T(8,128)(2,1)} %get-tuple-element.183), channel_id=1, source_target_pairs={{0,1},{1,0},{2,3},{3,2},{4,5},{5,4},{6,7},{7,6},{8,9},{9,8},{10,11... | collective-permute-start | bytes 2359304 | tf_op jit(solution)/shard_map/ppermute | solution.py:436
  140.1 53.7 %all-to-all-start.1 = ((bf16[32,64,384]{2,1,0:T(8,128)(2,1)}), bf16[32,64,384]{2,1,0:T(8,128)(2,1)S(1)}, u32[]{:S(2)}, u32[]{:S(2)}) async-start(bf16[32,64,384]{2,1,0:T(8,128)(2,1)} %copy_bitcast_fusion.29), calls=%async_computation.1 | async-start | bytes 3145728 | tf_op jit(solution)/shard_map/all_to_all | solution.py:444
  193.9 44.8 %all-to-all-start.2 = ((bf16[32,64,384]{2,1,0:T(8,128)(2,1)}), bf16[32,64,384]{2,1,0:T(8,128)(2,1)}, u32[]{:S(2)}, u32[]{:S(2)}) async-start(bf16[32,64,384]{2,1,0:T(8,128)(2,1)} %copy_bitcast_fusion.27), calls=%async_computation.2 | async-start | bytes 3145728 | tf_op jit(solution)/shard_map/all_to_all | solution.py:444
  238.6 42.0 %all-to-all-start.3 = ((bf16[32,64,384]{2,1,0:T(8,128)(2,1)}), bf16[32,64,384]{2,1,0:T(8,128)(2,1)}, u32[]{:S(2)}, u32[]{:S(2)}) async-start(bf16[32,64,384]{2,1,0:T(8,128)(2,1)} %copy_bitcast_fusion.25), calls=%async_computation.3 | async-start | bytes 3145728 | tf_op jit(solution)/shard_map/all_to_all | solution.py:444
  318.8 41.6 %all-to-all-start.5 = ((bf16[32,64,384]{2,1,0:T(8,128)(2,1)}), bf16[32,64,384]{2,1,0:T(8,128)(2,1)S(1)}, u32[]{:S(2)}, u32[]{:S(2)}) async-start(bf16[32,64,384]{2,1,0:T(8,128)(2,1)} %bitcast.328), calls=%async_computation.5 | async-start | bytes 3145728 | tf_op jit(solution)/shard_map/all_to_all | solution.py:444
  360.4 41.6 %all-to-all-start.7 = ((bf16[32,64,384]{2,1,0:T(8,128)(2,1)}), bf16[32,64,384]{2,1,0:T(8,128)(2,1)S(1)}, u32[]{:S(2)}, u32[]{:S(2)}) async-start(bf16[32,64,384]{2,1,0:T(8,128)(2,1)} %bitcast.341), calls=%async_computation.7 | async-start | bytes 3145728 | tf_op jit(solution)/shard_map/all_to_all | solution.py:444
  403.2 62.3 %all-to-all-start.4 = ((bf16[32,64,384]{2,1,0:T(8,128)(2,1)}), bf16[32,64,384]{2,1,0:T(8,128)(2,1)S(1)}, u32[]{:S(2)}, u32[]{:S(2)}) async-start(bf16[32,64,384]{2,1,0:T(8,128)(2,1)} %bitcast.340), calls=%async_computation.4 | async-start | bytes 3145728 | tf_op jit(solution)/shard_map/all_to_all | solution.py:444
  411.5 36.3 %collective-permute-start.29 = (bf16[8,192,256]{2,1,0:T(8,128)(2,1)}, bf16[8,192,256]{2,1,0:T(8,128)(2,1)}, u32[]{:S(2)}, u32[]{:S(2)}) collective-permute-start(bf16[8,192,256]{2,1,0:T(8,128)(2,1)} %get-tuple-element.169), channel_id=1, source_target_pairs={{0,3},{1,2},{2,1},{3,0},{4,7},{5,6},{6,5},{7,4},{8,11},{9,10},{10,... | collective-permute-start | bytes 2359304 | tf_op jit(solution)/shard_map/ppermute | solution.py:436
  414.3 48.2 %collective-permute-start.28 = (bf16[8,192,256]{2,1,0:T(8,128)(2,1)}, bf16[8,192,256]{2,1,0:T(8,128)(2,1)}, u32[]{:S(2)}, u32[]{:S(2)}) collective-permute-start(bf16[8,192,256]{2,1,0:T(8,128)(2,1)} %get-tuple-element.170), channel_id=1, source_target_pairs={{0,2},{1,3},{2,0},{3,1},{4,6},{5,7},{6,4},{7,5},{8,10},{9,11},{10,... | collective-permute-start | bytes 2359304 | tf_op jit(solution)/shard_map/ppermute | solution.py:436
  414.8 48.8 %collective-permute-start.27 = (bf16[8,192,256]{2,1,0:T(8,128)(2,1)}, bf16[8,192,256]{2,1,0:T(8,128)(2,1)}, u32[]{:S(2)}, u32[]{:S(2)}) collective-permute-start(bf16[8,192,256]{2,1,0:T(8,128)(2,1)} %get-tuple-element.171), channel_id=1, source_target_pairs={{0,1},{1,0},{2,3},{3,2},{4,5},{5,4},{6,7},{7,6},{8,9},{9,8},{10,11... | collective-permute-start | bytes 2359304 | tf_op jit(solution)/shard_map/ppermute | solution.py:436
  415.0 104.1 %collective-permute-start.17 = (bf16[8,192,256]{2,1,0:T(8,128)(2,1)}, bf16[8,192,256]{2,1,0:T(8,128)(2,1)}, u32[]{:S(2)}, u32[]{:S(2)}) collective-permute-start(bf16[8,192,256]{2,1,0:T(8,128)(2,1)} %get-tuple-element.177), channel_id=1, source_target_pairs={{0,3},{1,2},{2,1},{3,0},{4,7},{5,6},{6,5},{7,4},{8,11},{9,10},{10,... | collective-permute-start | bytes 2359304 | tf_op jit(solution)/shard_map/ppermute | solution.py:436
  417.8 103.0 %collective-permute-start.16 = (bf16[8,192,256]{2,1,0:T(8,128)(2,1)}, bf16[8,192,256]{2,1,0:T(8,128)(2,1)}, u32[]{:S(2)}, u32[]{:S(2)}) collective-permute-start(bf16[8,192,256]{2,1,0:T(8,128)(2,1)} %get-tuple-element.178), channel_id=1, source_target_pairs={{0,2},{1,3},{2,0},{3,1},{4,6},{5,7},{6,4},{7,5},{8,10},{9,11},{10,... | collective-permute-start | bytes 2359304 | tf_op jit(solution)/shard_map/ppermute | solution.py:436
  447.8 74.4 %collective-permute-start.15 = (bf16[8,192,256]{2,1,0:T(8,128)(2,1)}, bf16[8,192,256]{2,1,0:T(8,128)(2,1)}, u32[]{:S(2)}, u32[]{:S(2)}) collective-permute-start(bf16[8,192,256]{2,1,0:T(8,128)(2,1)} %get-tuple-element.179), channel_id=1, source_target_pairs={{0,1},{1,0},{2,3},{3,2},{4,5},{5,4},{6,7},{7,6},{8,9},{9,8},{10,11... | collective-permute-start | bytes 2359304 | tf_op jit(solution)/shard_map/ppermute | solution.py:436
  462.5 134.5 %collective-permute-start.5 = (bf16[8,192,256]{2,1,0:T(8,128)(2,1)}, bf16[8,192,256]{2,1,0:T(8,128)(2,1)}, u32[]{:S(2)}, u32[]{:S(2)}) collective-permute-start(bf16[8,192,256]{2,1,0:T(8,128)(2,1)} %get-tuple-element.193), channel_id=1, source_target_pairs={{0,3},{1,2},{2,1},{3,0},{4,7},{5,6},{6,5},{7,4},{8,11},{9,10},{10,... | collective-permute-start | bytes 2359304 | tf_op jit(solution)/shard_map/ppermute | solution.py:436
  463.6 135.4 %collective-permute-start.26 = (bf16[8,192,256]{2,1,0:T(8,128)(2,1)}, bf16[8,192,256]{2,1,0:T(8,128)(2,1)}, u32[]{:S(2)}, u32[]{:S(2)}) collective-permute-start(bf16[8,192,256]{2,1,0:T(8,128)(2,1)} %get-tuple-element.173), channel_id=1, source_target_pairs={{0,3},{1,2},{2,1},{3,0},{4,7},{5,6},{6,5},{7,4},{8,11},{9,10},{10,... | collective-permute-start | bytes 2359304 | tf_op jit(solution)/shard_map/ppermute | solution.py:436
  466.6 81.7 %all-to-all-start.6 = ((bf16[32,64,384]{2,1,0:T(8,128)(2,1)}), bf16[32,64,384]{2,1,0:T(8,128)(2,1)}, u32[]{:S(2)}, u32[]{:S(2)}) async-start(bf16[32,64,384]{2,1,0:T(8,128)(2,1)} %bitcast.339), calls=%async_computation.6 | async-start | bytes 3145728 | tf_op jit(solution)/shard_map/all_to_all | solution.py:444
  519.1 88.4 %collective-permute-start.25 = (bf16[8,192,256]{2,1,0:T(8,128)(2,1)}, bf16[8,192,256]{2,1,0:T(8,128)(2,1)}, u32[]{:S(2)}, u32[]{:S(2)}) collective-permute-start(bf16[8,192,256]{2,1,0:T(8,128)(2,1)} %get-tuple-element.174), channel_id=1, source_target_pairs={{0,2},{1,3},{2,0},{3,1},{4,6},{5,7},{6,4},{7,5},{8,10},{9,11},{10,... | collective-permute-start | bytes 2359304 | tf_op jit(solution)/shard_map/ppermute | solution.py:436
  520.8 88.2 %collective-permute-start.24 = (bf16[8,192,256]{2,1,0:T(8,128)(2,1)}, bf16[8,192,256]{2,1,0:T(8,128)(2,1)}, u32[]{:S(2)}, u32[]{:S(2)}) collective-permute-start(bf16[8,192,256]{2,1,0:T(8,128)(2,1)} %get-tuple-element.175), channel_id=1, source_target_pairs={{0,1},{1,0},{2,3},{3,2},{4,5},{5,4},{6,7},{7,6},{8,9},{9,8},{10,11... | collective-permute-start | bytes 2359304 | tf_op jit(solution)/shard_map/ppermute | solution.py:436
  522.2 87.3 %collective-permute-start.30 = (bf16[8,192,256]{2,1,0:T(8,128)(2,1)}, bf16[8,192,256]{2,1,0:T(8,128)(2,1)S(1)}, u32[]{:S(2)}, u32[]{:S(2)}) collective-permute-start(bf16[8,192,256]{2,1,0:T(8,128)(2,1)} %get-tuple-element.101), channel_id=1, source_target_pairs={{1,0},{0,1},{3,2},{2,3},{5,4},{4,5},{7,6},{6,7},{9,8},{8,9},{11,10... | collective-permute-start | bytes 2359304 | tf_op jit(solution)/shard_map/ppermute | solution.py:441
  548.3 90.3 %all-to-all-start.9 = ((bf16[32,64,384]{2,1,0:T(8,128)(2,1)}), bf16[32,64,384]{2,1,0:T(8,128)(2,1)S(1)}, u32[]{:S(2)}, u32[]{:S(2)}) async-start(bf16[32,64,384]{2,1,0:T(8,128)(2,1)} %copy_bitcast_fusion.13), calls=%async_computation.9 | async-start | bytes 3145728 | tf_op jit(solution)/shard_map/all_to_all | solution.py:444
  597.1 37.3 %collective-permute-start.31 = (bf16[8,192,256]{2,1,0:T(8,128)(2,1)S(1)}, bf16[8,192,256]{2,1,0:T(8,128)(2,1)S(1)}, u32[]{:S(2)}, u32[]{:S(2)}) collective-permute-start(bf16[8,192,256]{2,1,0:T(8,128)(2,1)S(1)} %copy-done.41), channel_id=1, source_target_pairs={{2,0},{3,1},{0,2},{1,3},{6,4},{7,5},{4,6},{5,7},{10,8},{11,9},{8,1... | collective-permute-start | bytes 2359304 | tf_op jit(solution)/shard_map/ppermute | solution.py:441
  599.0 37.2 %collective-permute-start.32 = (bf16[8,192,256]{2,1,0:T(8,128)(2,1)S(1)}, bf16[8,192,256]{2,1,0:T(8,128)(2,1)S(1)}, u32[]{:S(2)}, u32[]{:S(2)}) collective-permute-start(bf16[8,192,256]{2,1,0:T(8,128)(2,1)S(1)} %copy-done.40), channel_id=1, source_target_pairs={{3,0},{2,1},{1,2},{0,3},{7,4},{6,5},{5,6},{4,7},{11,8},{10,9},{9,1... | collective-permute-start | bytes 2359304 | tf_op jit(solution)/shard_map/ppermute | solution.py:441
  607.5 99.7 %collective-permute-start.4 = (bf16[8,192,256]{2,1,0:T(8,128)(2,1)}, bf16[8,192,256]{2,1,0:T(8,128)(2,1)}, u32[]{:S(2)}, u32[]{:S(2)}) collective-permute-start(bf16[8,192,256]{2,1,0:T(8,128)(2,1)} %get-tuple-element.194), channel_id=1, source_target_pairs={{0,2},{1,3},{2,0},{3,1},{4,6},{5,7},{6,4},{7,5},{8,10},{9,11},{10,... | collective-permute-start | bytes 2359304 | tf_op jit(solution)/shard_map/ppermute | solution.py:436
  608.9 98.2 %collective-permute-start.3 = (bf16[8,192,256]{2,1,0:T(8,128)(2,1)}, bf16[8,192,256]{2,1,0:T(8,128)(2,1)}, u32[]{:S(2)}, u32[]{:S(2)}) collective-permute-start(bf16[8,192,256]{2,1,0:T(8,128)(2,1)} %get-tuple-element.195), channel_id=1, source_target_pairs={{0,1},{1,0},{2,3},{3,2},{4,5},{5,4},{6,7},{7,6},{8,9},{9,8},{10,11... | collective-permute-start | bytes 2359304 | tf_op jit(solution)/shard_map/ppermute | solution.py:436
  609.5 97.7 %collective-permute-start.18 = (bf16[8,192,256]{2,1,0:T(8,128)(2,1)}, bf16[8,192,256]{2,1,0:T(8,128)(2,1)}, u32[]{:S(2)}, u32[]{:S(2)}) collective-permute-start(bf16[8,192,256]{2,1,0:T(8,128)(2,1)} %get-tuple-element.90), channel_id=1, source_target_pairs={{1,0},{0,1},{3,2},{2,3},{5,4},{4,5},{7,6},{6,7},{9,8},{8,9},{11,10... | collective-permute-start | bytes 2359304 | tf_op jit(solution)/shard_map/ppermute | solution.py:441
  634.4 72.8 %collective-permute-start.19 = (bf16[8,192,256]{2,1,0:T(8,128)(2,1)}, bf16[8,192,256]{2,1,0:T(8,128)(2,1)}, u32[]{:S(2)}, u32[]{:S(2)}) collective-permute-start(bf16[8,192,256]{2,1,0:T(8,128)(2,1)} %get-tuple-element.91), channel_id=1, source_target_pairs={{2,0},{3,1},{0,2},{1,3},{6,4},{7,5},{4,6},{5,7},{10,8},{11,9},{8,1... | collective-permute-start | bytes 2359304 | tf_op jit(solution)/shard_map/ppermute | solution.py:441
  637.2 70.0 %collective-permute-start.20 = (bf16[8,192,256]{2,1,0:T(8,128)(2,1)}, bf16[8,192,256]{2,1,0:T(8,128)(2,1)}, u32[]{:S(2)}, u32[]{:S(2)}) collective-permute-start(bf16[8,192,256]{2,1,0:T(8,128)(2,1)} %get-tuple-element.92), channel_id=1, source_target_pairs={{3,0},{2,1},{1,2},{0,3},{7,4},{6,5},{5,6},{4,7},{11,8},{10,9},{9,1... | collective-permute-start | bytes 2359304 | tf_op jit(solution)/shard_map/ppermute | solution.py:441
  639.8 60.9 %all-to-all-start.8 = ((bf16[32,64,384]{2,1,0:T(8,128)(2,1)}), bf16[32,64,384]{2,1,0:T(8,128)(2,1)S(1)}, u32[]{:S(2)}, u32[]{:S(2)}) async-start(bf16[32,64,384]{2,1,0:T(8,128)(2,1)} %copy_bitcast_fusion.15), calls=%async_computation.8 | async-start | bytes 3145728 | tf_op jit(solution)/shard_map/all_to_all | solution.py:444
  700.7 52.4 %all-to-all-start.11 = ((bf16[32,64,384]{2,1,0:T(8,128)(2,1)}), bf16[32,64,384]{2,1,0:T(8,128)(2,1)S(1)}, u32[]{:S(2)}, u32[]{:S(2)}) async-start(bf16[32,64,384]{2,1,0:T(8,128)(2,1)} %copy_bitcast_fusion.9), calls=%async_computation.11 | async-start | bytes 3145728 | tf_op jit(solution)/shard_map/all_to_all | solution.py:444
  753.1 43.6 %all-to-all-start.10 = ((bf16[32,64,384]{2,1,0:T(8,128)(2,1)}), bf16[32,64,384]{2,1,0:T(8,128)(2,1)}, u32[]{:S(2)}, u32[]{:S(2)}) async-start(bf16[32,64,384]{2,1,0:T(8,128)(2,1)} %copy_bitcast_fusion.11), calls=%async_computation.10 | async-start | bytes 3145728 | tf_op jit(solution)/shard_map/all_to_all | solution.py:444
  762.4 37.1 %collective-permute-start.33 = (bf16[8,192,256]{2,1,0:T(8,128)(2,1)}, bf16[8,192,256]{2,1,0:T(8,128)(2,1)}, u32[]{:S(2)}, u32[]{:S(2)}) collective-permute-start(bf16[8,192,256]{2,1,0:T(8,128)(2,1)} %get-tuple-element.105), channel_id=1, source_target_pairs={{1,0},{0,1},{3,2},{2,3},{5,4},{4,5},{7,6},{6,7},{9,8},{8,9},{11,10... | collective-permute-start | bytes 2359304 | tf_op jit(solution)/shard_map/ppermute | solution.py:441
  764.2 78.4 %collective-permute-start.34 = (bf16[8,192,256]{2,1,0:T(8,128)(2,1)}, bf16[8,192,256]{2,1,0:T(8,128)(2,1)}, u32[]{:S(2)}, u32[]{:S(2)}) collective-permute-start(bf16[8,192,256]{2,1,0:T(8,128)(2,1)} %get-tuple-element.106), channel_id=1, source_target_pairs={{2,0},{3,1},{0,2},{1,3},{6,4},{7,5},{4,6},{5,7},{10,8},{11,9},{8,1... | collective-permute-start | bytes 2359304 | tf_op jit(solution)/shard_map/ppermute | solution.py:441
  765.7 76.9 %collective-permute-start.35 = (bf16[8,192,256]{2,1,0:T(8,128)(2,1)}, bf16[8,192,256]{2,1,0:T(8,128)(2,1)}, u32[]{:S(2)}, u32[]{:S(2)}) collective-permute-start(bf16[8,192,256]{2,1,0:T(8,128)(2,1)} %get-tuple-element.107), channel_id=1, source_target_pairs={{3,0},{2,1},{1,2},{0,3},{7,4},{6,5},{5,6},{4,7},{11,8},{10,9},{9,1... | collective-permute-start | bytes 2359304 | tf_op jit(solution)/shard_map/ppermute | solution.py:441
  766.0 76.6 %collective-permute-start.21 = (bf16[8,192,256]{2,1,0:T(8,128)(2,1)}, bf16[8,192,256]{2,1,0:T(8,128)(2,1)}, u32[]{:S(2)}, u32[]{:S(2)}) collective-permute-start(bf16[8,192,256]{2,1,0:T(8,128)(2,1)} %get-tuple-element.94), channel_id=1, source_target_pairs={{1,0},{0,1},{3,2},{2,3},{5,4},{4,5},{7,6},{6,7},{9,8},{8,9},{11,10... | collective-permute-start | bytes 2359304 | tf_op jit(solution)/shard_map/ppermute | solution.py:441
  767.7 74.9 %collective-permute-start.22 = (bf16[8,192,256]{2,1,0:T(8,128)(2,1)}, bf16[8,192,256]{2,1,0:T(8,128)(2,1)}, u32[]{:S(2)}, u32[]{:S(2)}) collective-permute-start(bf16[8,192,256]{2,1,0:T(8,128)(2,1)} %get-tuple-element.95), channel_id=1, source_target_pairs={{2,0},{3,1},{0,2},{1,3},{6,4},{7,5},{4,6},{5,7},{10,8},{11,9},{8,1... | collective-permute-start | bytes 2359304 | tf_op jit(solution)/shard_map/ppermute | solution.py:441
  799.5 48.9 %collective-permute-start.23 = (bf16[8,192,256]{2,1,0:T(8,128)(2,1)S(1)}, bf16[8,192,256]{2,1,0:T(8,128)(2,1)S(1)}, u32[]{:S(2)}, u32[]{:S(2)}) collective-permute-start(bf16[8,192,256]{2,1,0:T(8,128)(2,1)S(1)} %copy-done.36), channel_id=1, source_target_pairs={{3,0},{2,1},{1,2},{0,3},{7,4},{6,5},{5,6},{4,7},{11,8},{10,9},{9,1... | collective-permute-start | bytes 2359304 | tf_op jit(solution)/shard_map/ppermute | solution.py:441
  839.4 40.1 %all-to-all-start.12 = ((bf16[32,64,384]{2,1,0:T(8,128)(2,1)}), bf16[32,64,384]{2,1,0:T(8,128)(2,1)S(1)}, u32[]{:S(2)}, u32[]{:S(2)}) async-start(bf16[32,64,384]{2,1,0:T(8,128)(2,1)} %bitcast.321), calls=%async_computation.12 | async-start | bytes 3145728 | tf_op jit(solution)/shard_map/all_to_all | solution.py:444
  842.1 212.6 %all-reduce.11.cloned.1.call-start = ((), (), s32[]{:S(2)}) async-start(), calls=%async_computation.16 | async-start | bytes 3743744 | tf_op jit(solution)/shard_map/psum | solution.py:581
  879.6 49.1 %all-to-all-start.14 = ((bf16[32,64,384]{2,1,0:T(8,128)(2,1)}), bf16[32,64,384]{2,1,0:T(8,128)(2,1)S(1)}, u32[]{:S(2)}, u32[]{:S(2)}) async-start(bf16[32,64,384]{2,1,0:T(8,128)(2,1)} %bitcast.319), calls=%async_computation.14 | async-start | bytes 3145728 | tf_op jit(solution)/shard_map/all_to_all | solution.py:444
  896.5 119.9 %collective-permute-start.36 = (bf16[8,192,256]{2,1,0:T(8,128)(2,1)}, bf16[8,192,256]{2,1,0:T(8,128)(2,1)}, u32[]{:S(2)}, u32[]{:S(2)}) collective-permute-start(bf16[8,192,256]{2,1,0:T(8,128)(2,1)} %get-tuple-element.119), channel_id=1, source_target_pairs={{1,0},{0,1},{3,2},{2,3},{5,4},{4,5},{7,6},{6,7},{9,8},{8,9},{11,10... | collective-permute-start | bytes 2359304 | tf_op jit(solution)/shard_map/ppermute | solution.py:441
  898.4 165.1 %collective-permute-start.37 = (bf16[8,192,256]{2,1,0:T(8,128)(2,1)}, bf16[8,192,256]{2,1,0:T(8,128)(2,1)}, u32[]{:S(2)}, u32[]{:S(2)}) collective-permute-start(bf16[8,192,256]{2,1,0:T(8,128)(2,1)} %get-tuple-element.120), channel_id=1, source_target_pairs={{2,0},{3,1},{0,2},{1,3},{6,4},{7,5},{4,6},{5,7},{10,8},{11,9},{8,1... | collective-permute-start | bytes 2359304 | tf_op jit(solution)/shard_map/ppermute | solution.py:441
  928.7 43.1 %all-to-all-start.13 = ((bf16[32,64,384]{2,1,0:T(8,128)(2,1)}), bf16[32,64,384]{2,1,0:T(8,128)(2,1)S(1)}, u32[]{:S(2)}, u32[]{:S(2)}) async-start(bf16[32,64,384]{2,1,0:T(8,128)(2,1)} %bitcast.320), calls=%async_computation.13 | async-start | bytes 3145728 | tf_op jit(solution)/shard_map/all_to_all | solution.py:444
  945.3 73.4 %collective-permute-start.42 = (bf16[8,192,256]{2,1,0:T(8,128)(2,1)}, bf16[8,192,256]{2,1,0:T(8,128)(2,1)}, u32[]{:S(2)}, u32[]{:S(2)}) collective-permute-start(bf16[8,192,256]{2,1,0:T(8,128)(2,1)} %get-tuple-element.131), channel_id=1, source_target_pairs={{1,0},{0,1},{3,2},{2,3},{5,4},{4,5},{7,6},{6,7},{9,8},{8,9},{11,10... | collective-permute-start | bytes 2359304 | tf_op jit(solution)/shard_map/ppermute | solution.py:441
  947.1 72.2 %collective-permute-start.43 = (bf16[8,192,256]{2,1,0:T(8,128)(2,1)}, bf16[8,192,256]{2,1,0:T(8,128)(2,1)}, u32[]{:S(2)}, u32[]{:S(2)}) collective-permute-start(bf16[8,192,256]{2,1,0:T(8,128)(2,1)} %get-tuple-element.132), channel_id=1, source_target_pairs={{2,0},{3,1},{0,2},{1,3},{6,4},{7,5},{4,6},{5,7},{10,8},{11,9},{8,1... | collective-permute-start | bytes 2359304 | tf_op jit(solution)/shard_map/ppermute | solution.py:441
  948.6 71.3 %collective-permute-start.44 = (bf16[8,192,256]{2,1,0:T(8,128)(2,1)}, bf16[8,192,256]{2,1,0:T(8,128)(2,1)}, u32[]{:S(2)}, u32[]{:S(2)}) collective-permute-start(bf16[8,192,256]{2,1,0:T(8,128)(2,1)} %get-tuple-element.133), channel_id=1, source_target_pairs={{3,0},{2,1},{1,2},{0,3},{7,4},{6,5},{5,6},{4,7},{11,8},{10,9},{9,1... | collective-permute-start | bytes 2359304 | tf_op jit(solution)/shard_map/ppermute | solution.py:441
  971.8 43.3 %all-to-all-start.15 = ((bf16[32,64,384]{2,1,0:T(8,128)(2,1)}), bf16[32,64,384]{2,1,0:T(8,128)(2,1)S(1)}, u32[]{:S(2)}, u32[]{:S(2)}) async-start(bf16[32,64,384]{2,1,0:T(8,128)(2,1)} %bitcast.318), calls=%async_computation.15 | async-start | bytes 3145728 | tf_op jit(solution)/shard_map/all_to_all | solution.py:444
  1016.4 49.8 %collective-permute-start.38 = (bf16[8,192,256]{2,1,0:T(8,128)(2,1)}, bf16[8,192,256]{2,1,0:T(8,128)(2,1)}, u32[]{:S(2)}, u32[]{:S(2)}) collective-permute-start(bf16[8,192,256]{2,1,0:T(8,128)(2,1)} %get-tuple-element.121), channel_id=1, source_target_pairs={{3,0},{2,1},{1,2},{0,3},{7,4},{6,5},{5,6},{4,7},{11,8},{10,9},{9,1... | collective-permute-start | bytes 2359304 | tf_op jit(solution)/shard_map/ppermute | solution.py:441
  1018.8 49.6 %collective-permute-start.39 = (bf16[8,192,256]{2,1,0:T(8,128)(2,1)}, bf16[8,192,256]{2,1,0:T(8,128)(2,1)}, u32[]{:S(2)}, u32[]{:S(2)}) collective-permute-start(bf16[8,192,256]{2,1,0:T(8,128)(2,1)} %get-tuple-element.125), channel_id=1, source_target_pairs={{1,0},{0,1},{3,2},{2,3},{5,4},{4,5},{7,6},{6,7},{9,8},{8,9},{11,10... | collective-permute-start | bytes 2359304 | tf_op jit(solution)/shard_map/ppermute | solution.py:441
  1019.3 49.0 %collective-permute-start.40 = (bf16[8,192,256]{2,1,0:T(8,128)(2,1)}, bf16[8,192,256]{2,1,0:T(8,128)(2,1)}, u32[]{:S(2)}, u32[]{:S(2)}) collective-permute-start(bf16[8,192,256]{2,1,0:T(8,128)(2,1)} %get-tuple-element.126), channel_id=1, source_target_pairs={{2,0},{3,1},{0,2},{1,3},{6,4},{7,5},{4,6},{5,7},{10,8},{11,9},{8,1... | collective-permute-start | bytes 2359304 | tf_op jit(solution)/shard_map/ppermute | solution.py:441
  1019.9 55.9 %collective-permute-start.41 = (bf16[8,192,256]{2,1,0:T(8,128)(2,1)}, bf16[8,192,256]{2,1,0:T(8,128)(2,1)}, u32[]{:S(2)}, u32[]{:S(2)}) collective-permute-start(bf16[8,192,256]{2,1,0:T(8,128)(2,1)} %get-tuple-element.127), channel_id=1, source_target_pairs={{3,0},{2,1},{1,2},{0,3},{7,4},{6,5},{5,6},{4,7},{11,8},{10,9},{9,1... | collective-permute-start | bytes 2359304 | tf_op jit(solution)/shard_map/ppermute | solution.py:441
  1063.4 29.6 %collective-permute-start.45 = (bf16[8,192,256]{2,1,0:T(8,128)(2,1)}, bf16[8,192,256]{2,1,0:T(8,128)(2,1)S(1)}, u32[]{:S(2)}, u32[]{:S(2)}) collective-permute-start(bf16[8,192,256]{2,1,0:T(8,128)(2,1)} %get-tuple-element.137), channel_id=1, source_target_pairs={{1,0},{0,1},{3,2},{2,3},{5,4},{4,5},{7,6},{6,7},{9,8},{8,9},{11,10... | collective-permute-start | bytes 2359304 | tf_op jit(solution)/shard_map/ppermute | solution.py:441
  1068.3 39.7 %collective-permute-start.47 = (bf16[8,192,256]{2,1,0:T(8,128)(2,1)S(1)}, bf16[8,192,256]{2,1,0:T(8,128)(2,1)S(1)}, u32[]{:S(2)}, u32[]{:S(2)}) collective-permute-start(bf16[8,192,256]{2,1,0:T(8,128)(2,1)S(1)} %copy-done.38), channel_id=1, source_target_pairs={{3,0},{2,1},{1,2},{0,3},{7,4},{6,5},{5,6},{4,7},{11,8},{10,9},{9,1... | collective-permute-start | bytes 2359304 | tf_op jit(solution)/shard_map/ppermute | solution.py:441
  (43 other events, 374.2 us)
Sparse Core Ops, SparseCore 0:
  868.0 186.6 all-reduce.10
